TPU v7x, 128 devices: a whole 4x4x4 slice. The times are simulated.
128 devices in a mesh: head: 2 (over core), inner: 8 (over y_hi, z), outer: 8 (over y_lo, x).
Axes of the slice: x: 4, y: 4 (y_hi: 2, y_lo: 2; y = y_hi * 2 + y_lo), z: 4, core: 2. Of those that a mesh axis runs over, the one named last changes fastest.
Arguments:
- query_vectors: bfloat16 [8192, 2048], P(('inner', 'outer'), 'head'), may hold values from -5 to 5
- window_keys: bfloat16 [16384, 256], P(('head', 'inner', 'outer')), may hold values from -6 to 6
- window_values: bfloat16 [16384, 256], P(('head', 'inner', 'outer')), may hold values from -6 to 6
- attention_output: bfloat16 [8192, 2048], P(('inner', 'outer'), 'head'), may hold values from -4 to 4
- output_gradient: bfloat16 [8192, 2048], P(('inner', 'outer'), 'head'), may hold values from -96 to 96
- query_blocks: int32 [64], replicated, may hold values from 0 to 63, as said below
- key_blocks: int32 [128], replicated, may hold values from 0 to 127, as said below
- kept_blocks: int32 [64, 64], replicated, may hold values from -1 to 127, as said below
Outputs:
- query_gradient: bfloat16 [8192, 2048], P(('inner', 'outer'), 'head')
- key_gradient: bfloat16 [16384, 256], P(('head', 'inner', 'outer'))
- value_gradient: bfloat16 [16384, 256], P(('head', 'inner', 'outer'))
Inputs may be any that keep to these rules, and one draw needn't show every extreme that they name: `query_blocks`: stored query blocks 2m and 2m + 1 hold slab positions p and 63 - p; every position once. `key_blocks`: stored key blocks 2m and 2m + 1 hold window positions p and 127 - p; every position once. `kept_blocks`: row b holds distinct key block positions, none above 64 + b and always that one; unused entries are -1 and come after the used ones.
All inputs are finite; a program needn't handle non-finite values.
Results may differ from a plain program's by a relative error of at most 0.0049.
Values may be sent and summed in bfloat16 or wider, within the bound.
A program may use at most 64 MiB of HBM per device.

v0:
```python
import math

import jax
import jax.numpy as jnp
from jax import lax
from jax.sharding import PartitionSpec as P

HEAD_SIZE = 128
GROUP_HEADS = 8
BLOCK_TOKENS = 128


NEG_FILL = -1e30


def joined(value, axis, combine):
    everything = jax.tree.map(lambda part: lax.all_gather(part, axis), value)
    first = jax.tree.map(lambda part: part[0], everything)

    def turn(k, so_far):
        return combine(so_far, jax.tree.map(lambda part: part[k], everything))

    return lax.fori_loop(1, lax.axis_size(axis), turn, first)


def lookup(table_rows, wanted):
    matches = wanted[:, None] == jnp.arange(table_rows.shape[0], dtype=jnp.int32)[None, :]
    return jnp.sum(jnp.where(matches, table_rows[None, :], 0), axis=1)


def lookup_rows(table_rows, wanted):
    matches = wanted[:, None] == jnp.arange(table_rows.shape[0], dtype=jnp.int32)[None, :]
    return jnp.sum(jnp.where(matches[:, :, None], table_rows[None, :, :], 0), axis=1)


def block_layout(query_slots, key_positions_list, query_blocks, key_blocks, kept_blocks):
    first_key = key_blocks.shape[0] - query_blocks.shape[0]
    query_pos = lookup(query_blocks, query_slots)
    key_pos = lookup(key_blocks, key_positions_list)
    kept_rows = lookup_rows(kept_blocks, query_pos)
    block_mask = jnp.any(kept_rows[:, :, None] == key_pos[None, None, :], axis=1)
    offsets = jnp.arange(BLOCK_TOKENS, dtype=jnp.int32)
    query_tok = ((first_key + query_pos)[:, None] * BLOCK_TOKENS + offsets[None, :]).reshape(-1)
    key_tok = (key_pos[:, None] * BLOCK_TOKENS + offsets[None, :]).reshape(-1)
    return (block_mask, query_tok, key_tok)


def tile_mask(layout, query_start, key_start, query_span, key_span):
    block_mask, query_tok, key_tok = layout
    picked = lax.dynamic_slice(
        block_mask,
        (query_start // BLOCK_TOKENS, key_start // BLOCK_TOKENS),
        (query_span // BLOCK_TOKENS, key_span // BLOCK_TOKENS),
    )
    expanded = jnp.repeat(jnp.repeat(picked, BLOCK_TOKENS, axis=0), BLOCK_TOKENS, axis=1)
    rows_tok = lax.dynamic_slice_in_dim(query_tok, query_start, query_span)
    cols_tok = lax.dynamic_slice_in_dim(key_tok, key_start, key_span)
    return expanded & (cols_tok[None, :] <= rows_tok[:, None])


def scores_of(query_piece, key_tile):
    head_split = query_piece.reshape(query_piece.shape[0], GROUP_HEADS, HEAD_SIZE)
    product = jnp.einsum("qgd,kd->gqk", head_split, key_tile, preferred_element_type=jnp.float32)
    return product * (1.0 / math.sqrt(HEAD_SIZE))


def tile_plan(query_rows, key_rows):
    query_span = min(query_rows, 512)
    key_span = min(key_rows, 256)
    key_pieces = key_rows // key_span
    return (query_span, key_span, key_pieces, query_rows // query_span * key_pieces)


def row_statistics(group_queries, group_keys, layout):
    query_span, key_span, key_pieces, tile_count = tile_plan(
        group_queries.shape[0], group_keys.shape[0]
    )
    initial = (
        jnp.full((GROUP_HEADS, group_queries.shape[0]), NEG_FILL, jnp.float32),
        jnp.zeros((GROUP_HEADS, group_queries.shape[0]), jnp.float32),
    )

    def row_tile_step(tile_index, carried):
        query_start = tile_index // key_pieces * query_span
        key_start = tile_index % key_pieces * key_span
        allowed = tile_mask(layout, query_start, key_start, query_span, key_span)
        running_max, running_sum = carried
        query_piece = lax.dynamic_slice_in_dim(group_queries, query_start, query_span, 0)
        key_tile = lax.dynamic_slice_in_dim(group_keys, key_start, key_span, 0)
        scores = scores_of(query_piece, key_tile)
        tile_max = jnp.max(jnp.where(allowed[None], scores, NEG_FILL), axis=2)
        tile_sum = jnp.sum(
            jnp.exp(jnp.where(allowed[None], scores - tile_max[:, :, None], NEG_FILL)), axis=2
        )
        old_max = lax.dynamic_slice_in_dim(running_max, query_start, query_span, 1)
        old_sum = lax.dynamic_slice_in_dim(running_sum, query_start, query_span, 1)
        new_max = jnp.maximum(old_max, tile_max)
        new_sum = old_sum * jnp.exp(old_max - new_max) + tile_sum * jnp.exp(tile_max - new_max)
        return (
            lax.dynamic_update_slice_in_dim(running_max, new_max, query_start, 1),
            lax.dynamic_update_slice_in_dim(running_sum, new_sum, query_start, 1),
        )

    return lax.fori_loop(0, tile_count, row_tile_step, initial)


def gradients(group_queries, group_grads, group_keys, group_values, log_total, row_delta, layout):
    logit_scale = 1.0 / math.sqrt(HEAD_SIZE)
    query_rows = group_queries.shape[0]
    key_rows = group_keys.shape[0]
    query_span, key_span, key_pieces, tile_count = tile_plan(query_rows, key_rows)
    initial = (
        jnp.zeros((query_rows, GROUP_HEADS * HEAD_SIZE), jnp.float32),
        jnp.zeros((key_rows, HEAD_SIZE), jnp.float32),
        jnp.zeros((key_rows, HEAD_SIZE), jnp.float32),
    )

    def gradients_tile_step(tile_index, carried):
        query_start = tile_index // key_pieces * query_span
        key_start = tile_index % key_pieces * key_span
        allowed = tile_mask(layout, query_start, key_start, query_span, key_span)
        query_acc, key_acc, value_acc = carried
        query_piece = lax.dynamic_slice_in_dim(group_queries, query_start, query_span, 0)
        gradient_piece = lax.dynamic_slice_in_dim(group_grads, query_start, query_span, 0)
        key_tile = lax.dynamic_slice_in_dim(group_keys, key_start, key_span, 0)
        value_tile = lax.dynamic_slice_in_dim(group_values, key_start, key_span, 0)
        scores = scores_of(query_piece, key_tile)
        tile_total = lax.dynamic_slice_in_dim(log_total, query_start, query_span, 1)
        tile_delta = lax.dynamic_slice_in_dim(row_delta, query_start, query_span, 1)
        attn_probs = jnp.exp(jnp.where(allowed[None], scores - tile_total[:, :, None], NEG_FILL))
        probability_reduced = attn_probs.astype(jnp.bfloat16)
        grad_heads = gradient_piece.reshape(query_span, GROUP_HEADS, HEAD_SIZE)
        query_heads = query_piece.reshape(query_span, GROUP_HEADS, HEAD_SIZE)
        grad_probs = jnp.einsum(
            "qgd,kd->gqk", grad_heads, value_tile, preferred_element_type=jnp.float32
        )
        score_gradient = (attn_probs * (grad_probs - tile_delta[:, :, None])).astype(jnp.bfloat16)
        query_part = (
            jnp.einsum("gqk,kd->qgd", score_gradient, key_tile, preferred_element_type=jnp.float32)
            * logit_scale
        )
        key_part = (
            jnp.einsum(
                "gqk,qgd->kd", score_gradient, query_heads, preferred_element_type=jnp.float32
            )
            * logit_scale
        )
        value_part = jnp.einsum(
            "gqk,qgd->kd", probability_reduced, grad_heads, preferred_element_type=jnp.float32
        )
        old_query = lax.dynamic_slice_in_dim(query_acc, query_start, query_span, 0)
        old_key = lax.dynamic_slice_in_dim(key_acc, key_start, key_span, 0)
        old_value = lax.dynamic_slice_in_dim(value_acc, key_start, key_span, 0)
        return (
            lax.dynamic_update_slice_in_dim(
                query_acc,
                old_query + query_part.reshape(query_span, GROUP_HEADS * HEAD_SIZE),
                query_start,
                0,
            ),
            lax.dynamic_update_slice_in_dim(key_acc, old_key + key_part, key_start, 0),
            lax.dynamic_update_slice_in_dim(value_acc, old_value + value_part, key_start, 0),
        )

    return lax.fori_loop(0, tile_count, gradients_tile_step, initial)


def merge_rows(earlier, later):
    max_early, sum_early, delta_early = earlier
    max_late, sum_late, delta_late = later
    larger = jnp.maximum(max_early, max_late)
    total = sum_early * jnp.exp(max_early - larger) + sum_late * jnp.exp(max_late - larger)
    return (larger, total, delta_early + delta_late)


def body(
    query_vectors,
    window_keys,
    window_values,
    attention_output,
    output_gradient,
    query_blocks,
    key_blocks,
    kept_blocks,
):
    n_head = lax.axis_size("head")
    n_inner = lax.axis_size("inner")
    n_outer = lax.axis_size("outer")
    n_seq = n_inner * n_outer
    own_rows = query_vectors.shape[0]
    query_per = own_rows // BLOCK_TOKENS
    key_per = window_keys.shape[0] // BLOCK_TOKENS
    own_keys, own_values = (
        lax.all_to_all(window_keys, "head", split_axis=1, concat_axis=0, tiled=True),
        lax.all_to_all(window_values, "head", split_axis=1, concat_axis=0, tiled=True),
    )
    own_delta = jnp.einsum(
        "rgd,rgd->gr",
        output_gradient.reshape(own_rows, GROUP_HEADS, HEAD_SIZE),
        attention_output.reshape(own_rows, GROUP_HEADS, HEAD_SIZE),
        preferred_element_type=jnp.float32,
    )
    head_ids = jnp.arange(n_head, dtype=jnp.int32)
    block_ids = jnp.arange(query_per, dtype=jnp.int32)
    key_ids = jnp.arange(key_per, dtype=jnp.int32)
    row_group = lax.axis_index("inner")
    col_member = lax.axis_index("outer")
    group_queries, group_grads = (
        lax.all_gather(query_vectors, "outer", axis=0, tiled=True),
        lax.all_gather(output_gradient, "outer", axis=0, tiled=True),
    )
    group_keys, group_values = (
        lax.all_gather(own_keys, "inner", axis=0, tiled=True),
        lax.all_gather(own_values, "inner", axis=0, tiled=True),
    )
    members = jnp.arange(n_outer, dtype=jnp.int32)
    query_slots = (
        (row_group * n_outer + members)[:, None] * query_per + block_ids[None, :]
    ).reshape(-1)
    sources = jnp.arange(n_inner, dtype=jnp.int32)
    key_positions_list = (
        (head_ids[None, :, None] * n_seq + (sources * n_outer)[:, None, None] + col_member)
        * key_per
        + key_ids[None, None, :]
    ).reshape(-1)
    layout = block_layout(query_slots, key_positions_list, query_blocks, key_blocks, kept_blocks)
    running_max, running_sum = row_statistics(group_queries, group_keys, layout)
    delta_part = lax.dynamic_update_slice_in_dim(
        jnp.zeros((GROUP_HEADS, group_queries.shape[0]), jnp.float32),
        own_delta,
        col_member * own_rows,
        1,
    )
    group_max, group_sum, row_delta = joined(
        (running_max, running_sum, delta_part), "outer", merge_rows
    )
    log_total = group_max + jnp.log(group_sum)
    query_part, key_part, value_part = gradients(
        group_queries, group_grads, group_keys, group_values, log_total, row_delta, layout
    )
    query_own = lax.psum_scatter(query_part, "outer", scatter_dimension=0, tiled=True)
    key_own, value_own = (
        lax.psum_scatter(key_part, "inner", scatter_dimension=0, tiled=True),
        lax.psum_scatter(value_part, "inner", scatter_dimension=0, tiled=True),
    )
    key_gradient, value_gradient = (
        lax.all_to_all(
            key_own.astype(jnp.bfloat16), "head", split_axis=0, concat_axis=1, tiled=True
        ),
        lax.all_to_all(
            value_own.astype(jnp.bfloat16), "head", split_axis=0, concat_axis=1, tiled=True
        ),
    )
    return (query_own.astype(jnp.bfloat16), key_gradient, value_gradient)


def solution(mesh):
    placed = (
        P(("inner", "outer"), "head"),
        P(("head", "inner", "outer"), None),
        P(("head", "inner", "outer"), None),
        P(("inner", "outer"), "head"),
        P(("inner", "outer"), "head"),
        P(),
        P(),
        P(),
    )
    return jax.shard_map(
        body,
        mesh=mesh,
        in_specs=placed,
        out_specs=(
            P(("inner", "outer"), "head"),
            P(("head", "inner", "outer"), None),
            P(("head", "inner", "outer"), None),
        ),
        check_vma=False,
    )
```

profile of v0, /device:TPU:1, one launch (start us, length us, event | category | flops | bytes accessed | tf_op | source)
XLA Modules:
  0.0 821.5 jit_solution(9742593853319509467)
XLA Ops:
  9.7 4.7 all-to-all-start
  23.4 24.6 %all_gather.40 = f32[8,8,1024]{2,1,0:T(8,128)S(1)} all-gather(f32[1,8,1024]{2,1,0:T(8,128)S(1)} %bitcast_dynamic-update-slice_fusion), channel_id=1, replica_groups=mesh['head'=2,'inner'=8,'outer'=8] {'outer'}, dimensions={0}, use_global_device_ids=true | all-gather | bytes 294912 | tf_op jit(solution)/shard_map/all_gather | solution.py:17
  48.1 7.7 all-to-all-start.1
  55.8 39.3 %all_gather.32 = bf16[2048,128]{1,0:T(8,128)(2,1)} all-gather(bf16[256,128]{1,0:T(8,128)(2,1)S(1)} %bitcast.220), channel_id=1, replica_groups=mesh['head'=2,'inner'=8,'outer'=8] {'inner'}, dimensions={0}, use_global_device_ids=true | all-gather | bytes 589824 | tf_op jit(solution)/shard_map/all_gather | solution.py:213
  95.2 31.9 %all_gather.41 = bf16[2048,128]{1,0:T(8,128)(2,1)} all-gather(bf16[256,128]{1,0:T(8,128)(2,1)S(1)} %bitcast.221), channel_id=1, replica_groups=mesh['head'=2,'inner'=8,'outer'=8] {'inner'}, dimensions={0}, use_global_device_ids=true | all-gather | bytes 589824 | tf_op jit(solution)/shard_map/all_gather | solution.py:214
  127.1 72.4 %while.57 = (s32[]{:T(128)}, f32[8,1024]{1,0:T(8,128)S(1)}, f32[8,1024]{1,0:T(8,128)S(1)}, pred[8,16]{0,1:T(8,128)(4,1)S(1)}, s32[2048]{0:T(1024)S(1)}, /*index=...) while((s32[]{:T(128)}, f32[8,1024]{1,0:T(8,128)S(1)}, ...), condition=%wide.region_7.8_spmd, body=%wide.region_4.7_spmd.sunk | while | flops 276054080 | bytes 12154650 | solution.py:104
  199.5 22.5 %all-gather.1 = f32[64,1024]{1,0:T(8,128)S(1)} all-gather(f32[8,1024]{1,0:T(8,128)S(1)} %get-tuple-element.771), channel_id=3, replica_groups=mesh['head'=2,'inner'=8,'outer'=8] {'outer'}, dimensions={0}, use_global_device_ids=true | all-gather | bytes 294912 | tf_op jit(solution)/shard_map/all_gather | solution.py:17
  222.0 22.0 %all-gather = f32[64,1024]{1,0:T(8,128)S(1)} all-gather(f32[8,1024]{1,0:T(8,128)S(1)} %get-tuple-element.770), channel_id=2, replica_groups=mesh['head'=2,'inner'=8,'outer'=8] {'outer'}, dimensions={0}, use_global_device_ids=true | all-gather | bytes 294912 | tf_op jit(solution)/shard_map/all_gather | solution.py:17
  248.0 341.4 %while.59 = (s32[]{:T(128)}, f32[1024,1024]{1,0:T(8,128)}, f32[2048,128]{1,0:T(8,128)S(1)}, f32[2048,128]{1,0:T(8,128)}, bf16[2048,128]{1,0:T(8,128)(2,1)}, /*in...) while((s32[]{:T(128)}, f32[1024,1024]{1,0:T(8,128)}, ...), condition=%wide.region_11.12_spmd, body=%wide.region_10.11_spmd.sunk | while | flops 1354072064 | bytes 53671756 | solution.py:165
  248.5 3.2 constant_dynamic-slice_fusion.11
  291.2 3.2 constant_dynamic-slice_fusion.11
  312.6 3.2 constant_dynamic-slice_fusion.11
  334.0 3.2 constant_dynamic-slice_fusion.11
  355.4 3.2 constant_dynamic-slice_fusion.11
  398.1 3.2 constant_dynamic-slice_fusion.11
  419.4 3.2 constant_dynamic-slice_fusion.11
  440.7 3.2 constant_dynamic-slice_fusion.11
  462.1 3.2 constant_dynamic-slice_fusion.11
  483.4 3.2 constant_dynamic-slice_fusion.11
  591.6 90.7 %reduce-scatter.6.cloned.1.call-done = f32[256,128]{1,0:T(8,128)} async-done(((f32[2048,128]{1,0:T(8,128)}), f32[256,128]{1,0:T(8,128)}) %reduce-scatter.6.cloned.1.call-update) | async-done | bytes 131088 | tf_op jit(solution)/shard_map/reduce_scatter | solution.py:243
  683.2 6.0 all_to_all.76
  690.2 66.9 %reduce-scatter.8.cloned.1.call-done = f32[256,128]{1,0:T(8,128)} async-done(((f32[2048,128]{1,0:T(8,128)}), f32[256,128]{1,0:T(8,128)}) %reduce-scatter.8.cloned.1.call-update) | async-done | bytes 131088 | tf_op jit(solution)/shard_map/reduce_scatter | solution.py:244
  757.9 6.0 all_to_all.77
  764.8 48.4 %reduce-scatter.4.cloned.1.call-done = f32[128,1024]{1,0:T(8,128)} async-done(((f32[1024,1024]{1,0:T(8,128)}), f32[128,1024]{1,0:T(8,128)}) %reduce-scatter.4.cloned.1.call-update) | async-done | bytes 524304 | tf_op jit(solution)/shard_map/reduce_scatter | solution.py:241
  (508 shorter events, 402.0 us)
Async XLA Ops:
  7.2 1.9 copy-start
  7.2 119.9 %all-gather.5.cloned.1.call-start = ((), (), s32[]{:S(2)}) async-start(), calls=%async_computation.7 | async-start | bytes 2359296 | tf_op jit(solution)/shard_map/all_gather | solution.py:209
  9.7 38.4 %all-to-all-start = ((bf16[128,2,128]{2,0,1:T(8,128)(2,1)}), bf16[128,2,128]{2,0,1:T(8,128)(2,1)S(1)}, u32[]{:S(2)}, u32[]{:S(2)}) async-start(bf16[128,2,128]{2,0,1:T(8,128)(2,1)} %copy_bitcast_fusion.3), calls=%async_computation | async-start | bytes 131072 | tf_op jit(solution)/shard_map/all_to_all | solution.py:194
  14.4 230.1 %all-gather.7.cloned.1.call-start = ((), (), s32[]{:S(2)}) async-start(), calls=%async_computation.8 | async-start | bytes 2359296 | tf_op jit(solution)/shard_map/all_gather | solution.py:210
  48.1 47.1 %all-to-all-start.1 = ((bf16[128,2,128]{2,0,1:T(8,128)(2,1)}), bf16[128,2,128]{2,0,1:T(8,128)(2,1)S(1)}, u32[]{:S(2)}, u32[]{:S(2)}) async-start(bf16[128,2,128]{2,0,1:T(8,128)(2,1)} %copy_bitcast_fusion.2), calls=%async_computation.1 | async-start | bytes 131072 | tf_op jit(solution)/shard_map/all_to_all | solution.py:195
  55.8 626.5 %reduce-scatter.6.cloned.1.call-start = ((), (), s32[]{:S(2)}) async-start(), calls=%async_computation.10 | async-start | bytes 1179648 | tf_op jit(solution)/shard_map/reduce_scatter | solution.py:243
  589.4 1.0 copy-start.1
  590.4 166.6 %reduce-scatter.8.cloned.1.call-start = ((), (), s32[]{:S(2)}) async-start(), calls=%async_computation.11 | async-start | bytes 1179648 | tf_op jit(solution)/shard_map/reduce_scatter | solution.py:244
  591.0 222.2 %reduce-scatter.4.cloned.1.call-start = ((), (), s32[]{:S(2)}) async-start(), calls=%async_computation.9 | async-start | bytes 4718592 | tf_op jit(solution)/shard_map/reduce_scatter | solution.py:241
Sparse Core Ops, SparseCore 0:
  10.2 45.3 all-gather.4
  57.1 45.7 all-gather.6
  590.6 91.7 reduce-scatter.5
  686.2 70.7 reduce-scatter.7
  759.3 53.8 reduce-scatter.3
where the time goes:
time: 828 us; the launch traced here: 822 us
  local copies, waits for them, and re-layouts  209 us (25%)
  waiting for transfers between devices  207 us (25%)
  matrix products  167 us (20%)
  blocking collectives  152 us (18%)
  other arithmetic  56.7 us (7%)
  between operations  13.9 us (2%)
  starting transfers between devices  12.5 us (2%)
    reduce_scatter x1, waiting for transfers between devices, body(): lax.psum_scatter(key_part, 'inner', scatter_dimension=0, tiled=True)  90.7 us
    dynamic_slice x32, local copies, waits for them, and re-layouts, gradients_tile_step(): old_query = lax.dynamic_slice_in_dim(query_acc, query_start, query_span, 0)  82.5 us
    all_gather x3, blocking collectives, joined(): everything = jax.tree.map(lambda part: lax.all_gather(part, axis), value)  69.1 us
    reduce_scatter x1, waiting for transfers between devices, body(): lax.psum_scatter(value_part, 'inner', scatter_dimension=0, tiled=True)  66.9 us
    dynamic_update_slice x32, local copies, waits for them, and re-layouts, gradients_tile_step(): lax.dynamic_update_slice_in_dim(query_acc, old_query + query_part.reshape...  54.1 us
    dot_general x32, matrix products, scores_of(): jnp.einsum('qgd,kd->gqk', head_split, key_tile, preferred_element_type=jn...  52.4 us
    reduce_scatter x1, waiting for transfers between devices, body(): lax.psum_scatter(query_part, 'outer', scatter_dimension=0, tiled=True)  48.4 us
    dot_general x16, matrix products, gradients_tile_step(): jnp.einsum('gqk,qgd->kd', probability_reduced, grad_heads, preferred_elem...  44.3 us
  transfers between devices with their start and end apart: 7, of which 3 were waited for; matrix products, arithmetic and copies ran while one was open for 10% of the time, Pallas kernels for 0%

commit v1 on v0

v1 whole, which is shorter than its diff:
```python
import math

import jax
import jax.numpy as jnp
from jax import lax
from jax.experimental import pallas as pl
from jax.experimental.pallas import tpu as pltpu
from jax.sharding import PartitionSpec as P

HEADS = 8
D = 128
B = 128
RING = 4
LOCAL_KEYS = 32
ENTRIES = 64
FIRST_KEY = 64
SCALE = 1.0 / math.sqrt(D)
LOG2E = math.log2(math.e)
C2 = SCALE * LOG2E
NEG = -1e30
MASKED = -2e30
MESH = pl.DeviceIdType.MESH
ANY = pl.BlockSpec(memory_space=pl.ANY)
VMEM = pl.BlockSpec(memory_space=pltpu.VMEM)
SMEM = pl.BlockSpec(memory_space=pltpu.SMEM)
BF = jnp.bfloat16
F32 = jnp.float32


class Place:
    def __init__(self):
        self.h = lax.axis_index("head")
        inner, outer = lax.axis_index("inner"), lax.axis_index("outer")
        self.x, self.z = lax.rem(outer, 4), lax.rem(inner, 4)
        self.y = (inner // 4) * 2 + outer // 4

    def device(self, x=None, y=None, z=None, h=None):
        x, y, z, h = (
            own if new is None else new
            for own, new in ((self.x, x), (self.y, y), (self.z, z), (self.h, h))
        )
        return (h, (y // 2) * 4 + z, lax.rem(y, 2) * 4 + x)

    def along(self, axis, step):
        at = lax.rem(getattr(self, axis) + step + RING, RING)
        return self.device(**{axis: at})

    def partner(self):
        return self.device(h=1 - self.h)


def ring_at(me, step):
    return lax.rem(me + step + RING, RING)


def greet(devices):
    barrier = pltpu.get_barrier_semaphore()
    for device in devices:
        pl.semaphore_signal(barrier, inc=1, device_id=device, device_id_type=MESH)
    pl.semaphore_wait(barrier, len(devices))


class Gather:
    def __init__(self, place, axis, part, own, send, recv):
        self.me = getattr(place, axis)
        self.to = (place.along(axis, 1), place.along(axis, -1))
        self.part, self.own, self.send, self.recv = part, own, send, recv

    def copy(self, src, dst, way, k):
        return pltpu.make_async_remote_copy(
            src_ref=src,
            dst_ref=dst,
            send_sem=self.send.at[way * 3 + k],
            recv_sem=self.recv.at[way * 3 + k],
            device_id=self.to[way],
            device_id_type=MESH,
        )

    def start(self):
        for k in range(2):
            for way in range(2):
                for src, dst in self.own(k ^ way):
                    self.copy(src, dst, way, k).start()

    def whole(self, at, half, way, k):
        ref = self.part(at, half)
        return self.copy(ref, ref, way, k)

    def arrived(self, way, k):
        step = (-1 if way == 0 else 1) * (2 if k == 2 else 1)
        half = way if k == 2 else k ^ way
        self.whole(ring_at(self.me, step), half, way, k).wait_recv()

    def forward(self):
        for way in range(2):
            self.arrived(way, 0)
            step = -1 if way == 0 else 1
            self.whole(ring_at(self.me, step), way, way, 2).start()

    def finish(self):
        for way in range(2):
            self.arrived(way, 1)
        for way in range(2):
            self.arrived(way, 2)

    def sent(self):
        for way in range(2):
            for k in range(3):
                self.whole(self.me, k ^ way if k < 2 else way, way, k).wait_send()


def gather_kernel(
    q_ref, g_ref, k_ref, v_ref, qd_ref, kv_ref, local, swap_send, swap_recv, zs, zr, cs, cr
):
    place = Place()
    h, x, y, z = place.h, place.x, place.y, place.z
    greet(
        [place.along(a, s) for a in ("x", "y", "z") for s in (1, -1)] + [place.partner()]
    )
    partner = place.partner()
    theirs = pl.ds(pl.multiple_of((1 - h) * D, D), D)
    ours = pl.ds(pl.multiple_of(h * D, D), D)

    def swaps():
        return [
            pltpu.make_async_remote_copy(
                src_ref=source.at[:, theirs],
                dst_ref=kv_ref.at[1, x, y, n],
                send_sem=swap_send.at[n],
                recv_sem=swap_recv.at[n],
                device_id=partner,
                device_id_type=MESH,
            )
            for n, source in enumerate((k_ref, v_ref))
        ]

    for copy in swaps():
        copy.start()

    def own_qd(half):
        source = (q_ref, g_ref)[half]
        return [
            (source.at[:, a * D : (a + 1) * D], qd_ref.at[z, half, a]) for a in range(HEADS)
        ]

    gz = Gather(place, "z", lambda at, half: qd_ref.at[at, half], own_qd, zs, zr)
    gz.start()
    gx0 = Gather(
        place,
        "x",
        lambda at, half: kv_ref.at[0, y, at, half],
        lambda half: [((k_ref, v_ref)[half].at[:, ours], kv_ref.at[0, y, x, half])],
        cs.at[0],
        cr.at[0],
    )
    gx0.start()

    def own_copies():
        for n, source in enumerate((k_ref, v_ref)):
            yield pltpu.make_async_copy(source.at[:, ours], kv_ref.at[0, y, x, n], local.at[n])
        for half in range(2):
            for n, (src, dst) in enumerate(own_qd(half)):
                yield pltpu.make_async_copy(src, dst, local.at[2 + half * HEADS + n])

    own = list(own_copies())
    for copy in own:
        copy.start()

    def slab(n, line):
        return (
            lambda at, half: kv_ref.at[n, at, 2 * half : 2 * half + 2],
            lambda half: [
                (kv_ref.at[n, line, 2 * half : 2 * half + 2],) * 2
            ],
        )

    for copy in swaps():
        copy.wait_recv()
    gy1 = Gather(
        place,
        "y",
        lambda at, half: kv_ref.at[1, x, at, half],
        lambda half: [(kv_ref.at[1, x, y, half],) * 2],
        cs.at[1],
        cr.at[1],
    )
    gy1.start()
    gx0.forward()
    gy1.forward()
    gx0.finish()
    own[0].wait()
    own[1].wait()
    gy0 = Gather(place, "y", *slab(0, y), cs.at[2], cr.at[2])
    gy0.start()
    gy1.finish()
    gx1 = Gather(place, "x", *slab(1, x), cs.at[3], cr.at[3])
    gx1.start()
    gz.forward()
    gy0.forward()
    gx1.forward()
    gy0.finish()
    gx1.finish()
    gz.finish()
    for copy in own[2:]:
        copy.wait()
    for copy in swaps():
        copy.wait_send()
    for ring in (gz, gx0, gy1, gy0, gx1):
        ring.sent()


def gather(q, g, k, v):
    return pl.pallas_call(
        gather_kernel,
        out_shape=(
            jax.ShapeDtypeStruct((RING, 2, HEADS, B, D), BF),
            jax.ShapeDtypeStruct((2, RING, RING, 2, B, D), BF),
        ),
        in_specs=[ANY] * 4,
        out_specs=(ANY, ANY),
        scratch_shapes=[
            pltpu.SemaphoreType.DMA((2 + 2 * HEADS,)),
            pltpu.SemaphoreType.DMA((2,)),
            pltpu.SemaphoreType.DMA((2,)),
            pltpu.SemaphoreType.DMA((6,)),
            pltpu.SemaphoreType.DMA((6,)),
            pltpu.SemaphoreType.DMA((4, 6)),
            pltpu.SemaphoreType.DMA((4, 6)),
        ],
        compiler_params=pltpu.CompilerParams(collective_id=0, has_side_effects=True),
        name="gather",
    )(q, g, k, v)


def across(a, b):
    return lax.dot_general(a, b, (((1,), (1,)), ((), ())), preferred_element_type=F32)


def pick(list_ref, i, n):
    first = list_ref[i, 2 * n]
    second = list_ref[i, 2 * n + 1]
    return [(lax.rem(e, 64), (e // 64) * B - B) for e in (first, second)]


def allowed_of(gap, past):
    return gap <= past


def stats_kernel(
    qb_ref, kb_ref, kept_ref, qd_hbm, kv_hbm, o_hbm, st_ref, delta_ref, list_ref,
    q_vmem, k_vmem, g_vmem, o_vmem, m_ref, l_ref, place_ref, sems,
):
    place = Place()
    z = place.z
    loads = [
        pltpu.make_async_copy(qd_hbm.at[:, 0], q_vmem, sems.at[0]),
        pltpu.make_async_copy(kv_hbm.at[:, 0], k_vmem, sems.at[1]),
        pltpu.make_async_copy(qd_hbm.at[z, 1], g_vmem, sems.at[2]),
        pltpu.make_async_copy(o_hbm, o_vmem, sems.at[3]),
    ]
    for load in loads:
        load.start()

    def clear(n, _):
        place_ref[n] = -1
        return 0

    lax.fori_loop(0, 128, clear, 0, unroll=16)

    def enter(j, _):
        first, a, b = j // 16, lax.rem(j // 4, 4), lax.rem(j, 4)
        own = first == 0
        yy, xx = jnp.where(own, a, b), jnp.where(own, b, a)
        owner = jnp.where(own, place.h, 1 - place.h)
        slot = owner * 64 + (yy // 2) * 32 + z * 8 + lax.rem(yy, 2) * 4 + xx
        place_ref[kb_ref[slot]] = j
        return 0

    lax.fori_loop(0, LOCAL_KEYS, enter, 0, unroll=4)
    for i in range(RING):
        slot = (place.y // 2) * 32 + i * 8 + lax.rem(place.y, 2) * 4 + place.x
        position = qb_ref[slot]

        def more(state):
            e, _ = state
            return jnp.logical_and(e < ENTRIES, kept_ref[position, jnp.minimum(e, ENTRIES - 1)] >= 0)

        def step(state):
            e, count = state
            block = kept_ref[position, e]
            j = place_ref[block]
            list_ref[i, count] = j + jnp.where(block == FIRST_KEY + position, 64, 128)
            return e + 1, count + (j >= 0).astype(jnp.int32)

        _, count = lax.while_loop(more, step, (jnp.int32(0), jnp.int32(0)))
        list_ref[i, count] = 0
        list_ref[i, 34] = (count + 1) // 2

    for load in loads:
        load.wait()

    for a in range(HEADS):
        product = g_vmem[a].astype(F32) * o_vmem[:, a * D : (a + 1) * D].astype(F32)
        delta_ref[a : a + 1, :] = jnp.sum(jnp.transpose(product), axis=0, keepdims=True)

    gap = lax.broadcasted_iota(jnp.int32, (B, 2 * B), 0) - lax.rem(
        lax.broadcasted_iota(jnp.int32, (B, 2 * B), 1), B
    )
    m_ref[...] = jnp.full_like(m_ref, NEG)
    l_ref[...] = jnp.zeros_like(l_ref)
    for i in range(RING):

        def pair(n, _):
            (j0, past0), (j1, past1) = pick(list_ref, i, n)
            keys = jnp.concatenate([k_vmem[j0], k_vmem[j1]], axis=0)
            for c in range(HEADS // 2):
                queries = q_vmem[i, 2 * c : 2 * c + 2].reshape(2 * B, D)
                s = across(keys, queries)
                s = jnp.concatenate(
                    [
                        jnp.where(allowed_of(gap, past0), s[:B], MASKED),
                        jnp.where(allowed_of(gap, past1), s[B:], MASKED),
                    ],
                    axis=0,
                ).reshape(2 * B // 8, 8, 2 * B)
                old = m_ref[i, c]
                new = jnp.maximum(old, jnp.max(s, axis=0))
                m_ref[i, c] = new
                total = jnp.sum(jnp.exp2(s * C2 - (new * C2)[None]), axis=0)
                l_ref[i, c] = l_ref[i, c] * jnp.exp2((old - new) * C2) + total
            return 0

        lax.fori_loop(0, list_ref[i, 34], pair, 0)
    for i in range(RING):
        for c in range(HEADS // 2):
            m8 = m_ref[i, c]
            m = jnp.max(m8, axis=0, keepdims=True)
            l = jnp.sum(l_ref[i, c] * jnp.exp2((m8 - m) * C2), axis=0, keepdims=True)
            for t in range(2):
                row = pl.ds(2 * c + t, 1)
                st_ref[0, i, row, :] = m[:, t * B : (t + 1) * B]
                st_ref[1, i, row, :] = l[:, t * B : (t + 1) * B]


def statistics(qb, kb, kept, qd, kv, o):
    return pl.pallas_call(
        stats_kernel,
        out_shape=(
            jax.ShapeDtypeStruct((2, RING, HEADS, B), F32),
            jax.ShapeDtypeStruct((HEADS, B), F32),
            jax.ShapeDtypeStruct((RING, 40), jnp.int32),
        ),
        in_specs=[SMEM, SMEM, SMEM, ANY, ANY, ANY],
        out_specs=(VMEM, VMEM, SMEM),
        scratch_shapes=[
            pltpu.VMEM((RING, HEADS, B, D), BF),
            pltpu.VMEM((LOCAL_KEYS, B, D), BF),
            pltpu.VMEM((HEADS, B, D), BF),
            pltpu.VMEM((B, HEADS * D), BF),
            pltpu.VMEM((RING, HEADS // 2, 8, 2 * B), F32),
            pltpu.VMEM((RING, HEADS // 2, 8, 2 * B), F32),
            pltpu.SMEM((128,), jnp.int32),
            pltpu.SemaphoreType.DMA((4,)),
        ],
        compiler_params=pltpu.CompilerParams(vmem_limit_bytes=32 * 2**20),
        name="statistics",
    )(qb, kb, kept, qd, kv.reshape(LOCAL_KEYS, 2, B, D), o)


def exchange_kernel(st_ref, delta_ref, total_ref, all_delta_ref, sts, deltas, send, recv):
    place = Place()
    z = place.z
    greet([place.along("z", s) for s in (1, 2, 3)])

    def copies(step):
        to = place.along("z", step)
        for n, (src, dst) in enumerate(((st_ref, sts.at[step - 1]), (delta_ref, deltas.at[step - 1]))):
            yield pltpu.make_async_remote_copy(
                src_ref=src,
                dst_ref=dst,
                send_sem=send.at[step - 1, n],
                recv_sem=recv.at[step - 1, n],
                device_id=to,
                device_id_type=MESH,
            )

    for step in (2, 1, 3):
        for copy in copies(step):
            copy.start()
    for step in (1, 3, 2):
        for copy in copies(step):
            copy.wait()
    top = st_ref[0]
    for n in range(3):
        top = jnp.maximum(top, sts[n, 0])
    total = st_ref[1] * jnp.exp2((st_ref[0] - top) * C2)
    for n in range(3):
        total = total + sts[n, 1] * jnp.exp2((sts[n, 0] - top) * C2)
    total_ref[...] = top * C2 + jnp.log2(total)
    all_delta_ref[z] = delta_ref[...]
    for n in range(3):
        all_delta_ref[ring_at(z, -(n + 1))] = deltas[n]


def exchange(st, delta):
    return pl.pallas_call(
        exchange_kernel,
        out_shape=(
            jax.ShapeDtypeStruct((RING, HEADS, B), F32),
            jax.ShapeDtypeStruct((RING, HEADS, B), F32),
        ),
        in_specs=[VMEM, VMEM],
        out_specs=(VMEM, VMEM),
        scratch_shapes=[
            pltpu.VMEM((3, 2, RING, HEADS, B), F32),
            pltpu.VMEM((3, HEADS, B), F32),
            pltpu.SemaphoreType.DMA((3, 2)),
            pltpu.SemaphoreType.DMA((3, 2)),
        ],
        compiler_params=pltpu.CompilerParams(collective_id=1, has_side_effects=True),
        name="exchange",
    )(st, delta)


def grads_kernel(
    list_ref, qd_hbm, kv_hbm, total_ref, delta_ref, dq_ref, dkv_ref,
    qd_vmem, kv_vmem, dq_acc, dk_acc, dv_acc, sems,
):
    loads = [
        pltpu.make_async_copy(qd_hbm, qd_vmem, sems.at[0]),
        pltpu.make_async_copy(kv_hbm, kv_vmem, sems.at[1]),
    ]
    for load in loads:
        load.start()
    dk_acc[...] = jnp.zeros_like(dk_acc)
    dv_acc[...] = jnp.zeros_like(dv_acc)
    for load in loads:
        load.wait()
    gap = lax.broadcasted_iota(jnp.int32, (B, 2 * B), 0) - lax.rem(
        lax.broadcasted_iota(jnp.int32, (B, 2 * B), 1), B
    )
    for i in range(RING):
        dq_acc[...] = jnp.zeros_like(dq_acc)

        def pair(n, _):
            (j0, past0), (j1, past1) = pick(list_ref, i, n)
            keys = jnp.concatenate([kv_vmem[j0, 0], kv_vmem[j1, 0]], axis=0)
            values = jnp.concatenate([kv_vmem[j0, 1], kv_vmem[j1, 1]], axis=0)
            keys_t = jnp.transpose(keys)
            dk = jnp.zeros((2 * B, D), F32)
            dv = jnp.zeros((2 * B, D), F32)
            for c in range(HEADS // 2):
                queries = qd_vmem[i, 0, 2 * c : 2 * c + 2].reshape(2 * B, D)
                cotangents = qd_vmem[i, 1, 2 * c : 2 * c + 2].reshape(2 * B, D)
                total = jnp.concatenate(
                    [total_ref[i, 2 * c : 2 * c + 1, :], total_ref[i, 2 * c + 1 : 2 * c + 2, :]],
                    axis=1,
                )
                delta = jnp.concatenate(
                    [delta_ref[i, 2 * c : 2 * c + 1, :], delta_ref[i, 2 * c + 1 : 2 * c + 2, :]],
                    axis=1,
                )
                s = across(keys, queries)
                s = jnp.concatenate(
                    [
                        jnp.where(allowed_of(gap, past0), s[:B], MASKED),
                        jnp.where(allowed_of(gap, past1), s[B:], MASKED),
                    ],
                    axis=0,
                )
                p = jnp.exp2(s * C2 - total)
                ds = (p * (across(values, cotangents) - delta)).astype(BF)
                dv = dv + jnp.dot(p.astype(BF), cotangents, preferred_element_type=F32)
                dk = dk + jnp.dot(ds, queries, preferred_element_type=F32)
                cols = slice(2 * c * B, 2 * (c + 1) * B)
                dq_acc[:, cols] += jnp.dot(keys_t, ds, preferred_element_type=F32)
            dk_acc[j0] += dk[:B]
            dk_acc[j1] += dk[B:]
            dv_acc[j0] += dv[:B]
            dv_acc[j1] += dv[B:]
            return 0

        lax.fori_loop(0, list_ref[i, 34], pair, 0)
        dq_ref[i] = (dq_acc[...] * SCALE).astype(BF)
    for j in range(LOCAL_KEYS):
        dkv_ref[j, 0] = (dk_acc[j] * SCALE).astype(BF)
        dkv_ref[j, 1] = dv_acc[j].astype(BF)


def grads(lists, qd, kv, total, delta):
    return pl.pallas_call(
        grads_kernel,
        out_shape=(
            jax.ShapeDtypeStruct((RING, D, HEADS * B), BF),
            jax.ShapeDtypeStruct((LOCAL_KEYS, 2, B, D), BF),
        ),
        in_specs=[SMEM, ANY, ANY, VMEM, VMEM],
        out_specs=(VMEM, VMEM),
        scratch_shapes=[
            pltpu.VMEM((RING, 2, HEADS, B, D), BF),
            pltpu.VMEM((LOCAL_KEYS, 2, B, D), BF),
            pltpu.VMEM((D, HEADS * B), F32),
            pltpu.VMEM((LOCAL_KEYS, B, D), F32),
            pltpu.VMEM((LOCAL_KEYS, B, D), F32),
            pltpu.SemaphoreType.DMA((2,)),
        ],
        compiler_params=pltpu.CompilerParams(vmem_limit_bytes=48 * 2**20),
        name="grads",
    )(lists, qd, kv.reshape(LOCAL_KEYS, 2, B, D), total, delta)


class Scatter:
    def __init__(self, place, axis, part, near, far, mid, send, recv):
        self.me = getattr(place, axis)
        self.to = (place.along(axis, 1), place.along(axis, -1))
        self.part, self.near, self.far, self.mid = part, near, far, mid
        self.send, self.recv = send, recv

    def copy(self, src, dst, way, k):
        return pltpu.make_async_remote_copy(
            src_ref=src,
            dst_ref=dst,
            send_sem=self.send.at[way * 3 + k],
            recv_sem=self.recv.at[way * 3 + k],
            device_id=self.to[way],
            device_id_type=MESH,
        )

    def far_copy(self, way):
        return self.copy(self.part(ring_at(self.me, 2), way), self.far.at[way], way, 0)

    def plain_copy(self, way):
        step = 1 if way == 0 else -1
        return self.copy(self.part(ring_at(self.me, step), 1 - way), self.near(way, 1 - way), way, 1)

    def mid_copy(self, way):
        return self.copy(self.mid.at[way], self.near(way, way), way, 2)

    def start(self):
        for way in range(2):
            self.far_copy(way).start()
        for way in range(2):
            self.plain_copy(way).start()

    def forward(self):
        for way in range(2):
            step = 1 if way == 0 else -1
            self.far_copy(way).wait_recv()
            own = self.part(ring_at(self.me, step), way)[...].astype(F32)
            self.mid[way] = (self.far[way].astype(F32) + own).astype(BF)
            self.mid_copy(way).start()

    def finish(self):
        for way in range(2):
            self.plain_copy(way).wait_recv()
        for way in range(2):
            self.mid_copy(way).wait_recv()

    def half(self, half):
        total = self.part(self.me, half)[...].astype(F32)
        return total + self.near(0, half)[...].astype(F32) + self.near(1, half)[...].astype(F32)

    def sent(self):
        for way in range(2):
            self.far_copy(way).wait_send()
            self.plain_copy(way).wait_send()
            self.mid_copy(way).wait_send()


def scatter_kernel(
    dq_ref, dkv_ref, qg_ref, kg_ref, vg_ref,
    zn, zf, zm, n1, f1, m1, s1, n2, f2, m2, fin, qout, zs, zr, cs, cr, swap_send, swap_recv, local,
):
    place = Place()
    h, x, y, z = place.h, place.x, place.y, place.z
    greet(
        [place.along(a, s) for a in ("x", "y", "z") for s in (1, -1)] + [place.partner()]
    )
    width = HEADS * B // 2

    rz = Scatter(
        place,
        "z",
        lambda at, half: dq_ref.at[at, :, half * width : (half + 1) * width],
        lambda way, half: zn.at[way, half],
        zf, zm, zs, zr,
    )

    def first(n, axis):
        return Scatter(
            place,
            axis,
            lambda at, half: dkv_ref.at[n, at, 2 * half : 2 * half + 2],
            lambda way, half: n1.at[n, way, half],
            f1.at[n], m1.at[n], cs.at[n], cr.at[n],
        )

    def second(n, axis):
        return Scatter(
            place,
            axis,
            lambda at, half: s1.at[n, at, half],
            lambda way, half: n2.at[n, way, half],
            f2.at[n], m2.at[n], cs.at[2 + n], cr.at[2 + n],
        )

    ry0, rx1 = first(0, "y"), first(1, "x")
    rx0, ry1 = second(0, "x"), second(1, "y")
    ry0.start()
    rx1.start()
    rz.start()
    ry0.forward()
    rx1.forward()
    rz.forward()
    for n, (one, two) in enumerate(((ry0, rx0), (rx1, ry1))):
        one.finish()
        for half in range(2):
            s1[n, 2 * half : 2 * half + 2] = one.half(half).astype(BF)
        two.start()
    rx0.forward()
    ry1.forward()
    rz.finish()
    for half in range(2):
        total = rz.half(half)
        for a in range(HEADS // 2):
            head = half * (HEADS // 2) + a
            qout[:, head * D : (head + 1) * D] = jnp.transpose(
                total[:, a * B : (a + 1) * B]
            ).astype(BF)
    q_copy = pltpu.make_async_copy(qout, qg_ref, local.at[0])
    q_copy.start()
    ours = pl.ds(pl.multiple_of(h * D, D), D)
    ry1.finish()
    for half in range(2):
        fin[1, half] = ry1.half(half).astype(BF)
    swaps = [
        pltpu.make_async_remote_copy(
            src_ref=fin.at[1, n],
            dst_ref=target.at[:, ours],
            send_sem=swap_send.at[n],
            recv_sem=swap_recv.at[n],
            device_id=place.partner(),
            device_id_type=MESH,
        )
        for n, target in enumerate((kg_ref, vg_ref))
    ]
    for copy in swaps:
        copy.start()
    rx0.finish()
    for half in range(2):
        fin[0, half] = rx0.half(half).astype(BF)
    outs = [
        pltpu.make_async_copy(fin.at[0, n], target.at[:, ours], local.at[1 + n])
        for n, target in enumerate((kg_ref, vg_ref))
    ]
    for copy in outs:
        copy.start()
    for copy in outs:
        copy.wait()
    q_copy.wait()
    for copy in swaps:
        copy.wait()
    for ring in (rz, ry0, rx1, rx0, ry1):
        ring.sent()


def scatter(dq, dkv):
    half_block = (2, 2, B, D)
    return pl.pallas_call(
        scatter_kernel,
        out_shape=(
            jax.ShapeDtypeStruct((B, HEADS * D), BF),
            jax.ShapeDtypeStruct((B, 2 * D), BF),
            jax.ShapeDtypeStruct((B, 2 * D), BF),
        ),
        in_specs=[VMEM, VMEM],
        out_specs=(ANY, ANY, ANY),
        scratch_shapes=[
            pltpu.VMEM((2, 2, D, HEADS * B // 2), BF),
            pltpu.VMEM((2, D, HEADS * B // 2), BF),
            pltpu.VMEM((2, D, HEADS * B // 2), BF),
            pltpu.VMEM((2, 2, 2) + half_block, BF),
            pltpu.VMEM((2, 2) + half_block, BF),
            pltpu.VMEM((2, 2) + half_block, BF),
            pltpu.VMEM((2, RING, 2, B, D), BF),
            pltpu.VMEM((2, 2, 2, B, D), BF),
            pltpu.VMEM((2, 2, B, D), BF),
            pltpu.VMEM((2, 2, B, D), BF),
            pltpu.VMEM((2, 2, B, D), BF),
            pltpu.VMEM((B, HEADS * D), BF),
            pltpu.SemaphoreType.DMA((6,)),
            pltpu.SemaphoreType.DMA((6,)),
            pltpu.SemaphoreType.DMA((4, 6)),
            pltpu.SemaphoreType.DMA((4, 6)),
            pltpu.SemaphoreType.DMA((2,)),
            pltpu.SemaphoreType.DMA((2,)),
            pltpu.SemaphoreType.DMA((3,)),
        ],
        compiler_params=pltpu.CompilerParams(
            collective_id=2, has_side_effects=True, vmem_limit_bytes=32 * 2**20
        ),
        name="scatter",
    )(dq, dkv.reshape(2, RING, RING, 2, B, D))


def body(q, k, v, o, g, query_blocks, key_blocks, kept_blocks):
    qd, kv = gather(q, g, k, v)
    st, delta, lists = statistics(query_blocks, key_blocks, kept_blocks, qd, kv, o)
    total, all_delta = exchange(st, delta)
    dq, dkv = grads(lists, qd, kv, total, all_delta)
    return scatter(dq, dkv)


def solution(mesh):
    rows, stored = P(("inner", "outer"), "head"), P(("head", "inner", "outer"), None)
    return jax.shard_map(
        body,
        mesh=mesh,
        in_specs=(rows, stored, stored, rows, rows, P(), P(), P()),
        out_specs=(rows, stored, stored),
        check_vma=False,
    )
```

time: 828 us -> 92.4 us (0.11)
  waiting for transfers between devices: 207 us -> 0 us
  local copies, waits for them, and re-layouts: 209 us -> 10.8 us
  matrix products: 167 us -> 0 us
  blocking collectives: 152 us -> 0 us
  Pallas kernels: 0 us -> 80.4 us
  other arithmetic: 56.7 us -> 0 us
  between operations: 13.9 us -> 0.71 us
  starting transfers between devices: 12.5 us -> 0 us
    reduce_scatter x3 -> x0, waiting for transfers between devices: 206 us -> none  [the longest x1 90.7 us: body(): lax.psum_scatter(key_part, 'inner', scatter_dimension=0, tiled=True)]
    dot_general x96 -> x0, matrix products: 167 us -> none  [the longest x32 52.4 us: scores_of(): jnp.einsum('qgd,kd->gqk', head_split, key_tile, preferred_element_type=jn...]
    all_gather x5 -> x0, blocking collectives: 140 us -> none  [the longest x3 69.1 us: joined(): everything = jax.tree.map(lambda part: lax.all_gather(part, axis), value)]
    dynamic_slice x176 -> x0, local copies, waits for them, and re-layouts: 138 us -> none  [the longest x32 82.5 us: gradients_tile_step(): old_query = lax.dynamic_slice_in_dim(query_acc, query_start, query_span, 0)]
    pallas_call x0 -> x5, Pallas kernels: none -> 80.4 us  [the longest x1 26.4 us: gather(): pl.pallas_call(gather_kernel, out_shape=(jax.ShapeDtypeStruct((RING, 2, H...]
    dynamic_update_slice x33 -> x0, local copies, waits for them, and re-layouts: 54.1 us -> none  [the longest x32 54.1 us: gradients_tile_step(): lax.dynamic_update_slice_in_dim(query_acc, old_query + query_part.reshape...]
    add x28 -> x0, other arithmetic: 30.5 us -> none  [the longest x16 30.1 us: gradients_tile_step(): old_query + query_part.reshape(query_span, GROUP_HEADS * HEAD_SIZE)]
    reduce_sum x19 -> x0, other arithmetic: 16.7 us -> none  [the longest x16 14.1 us: row_tile_step(): jnp.sum(jnp.exp(jnp.where(allowed[None], scores - tile_max[:, :, None], N...]
  transfers between devices with their start and end apart: 7 -> 0, of which waited for: 3 -> 0; matrix products, arithmetic and copies ran while one was open for 10% -> 0% of each run, Pallas kernels for 0% -> 0%
where the time goes in v1:
time: 92.4 us; the launch traced here: 91.9 us
  Pallas kernels  80.4 us (87%)
  local copies, waits for them, and re-layouts  10.8 us (12%)
    pallas_call x1, Pallas kernels, gather(): pl.pallas_call(gather_kernel, out_shape=(jax.ShapeDtypeStruct((RING, 2, H...  26.4 us
    pallas_call x1, Pallas kernels, scatter(): pl.pallas_call(scatter_kernel, out_shape=(jax.ShapeDtypeStruct((B, HEADS...  21.8 us
    pallas_call x1, Pallas kernels, grads(): pl.pallas_call(grads_kernel, out_shape=(jax.ShapeDtypeStruct((RING, D, HE...  15.9 us
    unnamed x25, local copies, waits for them, and re-layouts  10.8 us
    pallas_call x1, Pallas kernels, statistics(): pl.pallas_call(stats_kernel, out_shape=(jax.ShapeDtypeStruct((2, RING, HE...  10.4 us
    pallas_call x1, Pallas kernels, exchange(): pl.pallas_call(exchange_kernel, out_shape=(jax.ShapeDtypeStruct((RING, HE...  5.91 us

profile of v1, /device:TPU:1, one launch (start us, length us, event | category | flops | bytes accessed | tf_op | source)
XLA Modules:
  0.0 91.9 jit_solution(6619930166784682334)
XLA Ops:
  0.6 26.4 %gather.1 = (bf16[4,2,8,128,128]{4,3,2,1,0:T(8,128)(2,1)}, bf16[2,4,4,2,128,128]{5,4,3,2,1,0:T(8,128)(2,1)}) custom-call(bf16[128,1024]{1,0:T(8,128)(2,1)} %q_ref.1, bf16[128,1024]{1,0:T(8,128)(2,1)} %g_ref.1, bf16[128,256]{1,0:T(8,128)(2,1)} %k_ref.1, bf16[128,256]{1,0:T(8,128)(2,1)} %v_ref.1), custom_call_target="tpu_custom_call" | custom-call | tf_op jit(solution)/shard_map/gather/pallas_call | solution.py:213
  27.1 0.0 copy-start
  27.1 1.6 %copy-done = bf16[4,2,8,128,128]{4,3,2,1,0:T(8,128)(2,1)S(1)} copy-done((bf16[4,2,8,128,128]{4,3,2,1,0:T(8,128)(2,1)S(1)}, bf16[4,2,8,128,128]{4,3,2,1,0:T(8,128)(2,1)}, u32[]{:S(2)}) %copy-start) | copy-done | bytes 2097176
  28.7 0.0 copy-start.2
  28.7 1.6 %copy-done.2 = bf16[2,4,4,2,128,128]{5,4,3,2,1,0:T(8,128)(2,1)S(1)} copy-done((bf16[2,4,4,2,128,128]{5,4,3,2,1,0:T(8,128)(2,1)S(1)}, bf16[2,4,4,2,128,128]{5,4,3,2,1,0:T(8,128)(2,1)}, u32[]{:S(2)}) %copy-start.2) | copy-done | bytes 2097176
  30.2 0.0 copy-start.3
  30.2 0.9 %copy-done.3 = bf16[128,1024]{1,0:T(8,128)(2,1)S(1)} copy-done((bf16[128,1024]{1,0:T(8,128)(2,1)S(1)}, bf16[128,1024]{1,0:T(8,128)(2,1)}, u32[]{:S(2)}) %copy-start.3) | copy-done | bytes 262168
  31.2 0.8 copy-done.4
  32.0 0.7 copy-done.9
  32.6 0.7 copy-done.10
  33.3 10.4 %statistics.1 = (f32[2,4,8,128]{3,2,1,0:T(8,128)S(1)}, f32[8,128]{1,0:T(8,128)S(1)}, s32[4,40]{1,0:T(4,128)S(1)}) custom-call(s32[64]{0:T(128)S(1)} %copy-done.9, s32[128]{0:T(128)S(1)} %copy-done.10, s32[64,64]{1,0:T(8,128)S(1)} %copy-done.4, bf16[4,2,8,128,128]{4,3,2,1,0:T(8,128)(2,1)S(1)} %copy-done, bf16[32,2,128,128]{3,2,1,0:T(8,128)(2,1)S(1)} %bitcast.3, ...), custom_call_target="tpu_custom_call" | custom-call | tf_op jit(solution)/shard_map/statistics/pallas_call | solution.py:346
  43.7 0.0 copy-start.5
  43.7 0.6 copy-done.5
  44.3 0.6 copy-done.8
  44.9 5.9 %exchange.1 = (f32[4,8,128]{2,1,0:T(8,128)}, f32[4,8,128]{2,1,0:T(8,128)}) custom-call(f32[2,4,8,128]{3,2,1,0:T(8,128)} %copy-done.5, f32[8,128]{1,0:T(8,128)} %copy-done.8), custom_call_target="tpu_custom_call" | custom-call | tf_op jit(solution)/shard_map/exchange/pallas_call | solution.py:406
  50.8 0.0 copy-done.1
  50.8 0.0 copy-start.6
  50.8 0.7 copy-done.6
  51.5 0.7 copy-done.7
  52.2 15.9 %grads.1 = (bf16[4,128,1024]{2,1,0:T(8,128)(2,1)S(1)}, bf16[32,2,128,128]{3,2,1,0:T(8,128)(2,1)S(1)}) custom-call(s32[4,40]{1,0:T(4,128)S(1)} %get-tuple-element.14.list_ref, bf16[4,2,8,128,128]{4,3,2,1,0:T(8,128)(2,1)S(1)} %copy-done.1, bf16[32,2,128,128]{3,2,1,0:T(8,128)(2,1)} %bitcast.2, f32[4,8,128]{2,1,0:T(8,128)S(1)} %copy-done.6, ...), custom_call_target="tpu_custom_call" | custom-call | tf_op jit(solution)/shard_map/grads/pallas_call | solution.py:491
  68.2 21.8 %scatter.1 = (bf16[128,1024]{1,0:T(8,128)(2,1)S(1)}, bf16[128,256]{1,0:T(8,128)(2,1)S(1)}, bf16[128,256]{1,0:T(8,128)(2,1)S(1)}) custom-call(bf16[4,128,1024]{2,1,0:T(8,128)(2,1)S(1)} %get-tuple-element.19.dq_ref, bf16[2,4,4,2,128,128]{5,4,3,2,1,0:T(8,128)(2,1)S(1)} %bitcast.4), custom_call_target="tpu_custom_call" | custom-call | tf_op jit(solution)/shard_map/scatter/pallas_call | solution.py:669
  90.0 0.7 copy.14
  90.7 0.6 copy.15
  91.3 0.6 copy.16
  (6 shorter events, 0.0 us)
Async XLA Ops:
  27.1 1.6 %copy-start = (bf16[4,2,8,128,128]{4,3,2,1,0:T(8,128)(2,1)S(1)}, bf16[4,2,8,128,128]{4,3,2,1,0:T(8,128)(2,1)}, u32[]{:S(2)}) copy-start(bf16[4,2,8,128,128]{4,3,2,1,0:T(8,128)(2,1)} %get-tuple-element.12.qd_hbm) | copy-start | bytes 6291460
  28.7 1.6 %copy-start.2 = (bf16[2,4,4,2,128,128]{5,4,3,2,1,0:T(8,128)(2,1)S(1)}, bf16[2,4,4,2,128,128]{5,4,3,2,1,0:T(8,128)(2,1)}, u32[]{:S(2)}) copy-start(bf16[2,4,4,2,128,128]{5,4,3,2,1,0:T(8,128)(2,1)} %get-tuple-element.13) | copy-start | bytes 6291460
  30.2 0.9 %copy-start.3 = (bf16[128,1024]{1,0:T(8,128)(2,1)S(1)}, bf16[128,1024]{1,0:T(8,128)(2,1)}, u32[]{:S(2)}) copy-start(bf16[128,1024]{1,0:T(8,128)(2,1)} %o_hbm.1) | copy-start | bytes 786436
  31.2 0.8 copy-start.4
  32.0 0.7 copy-start.9
  32.6 0.7 copy-start.10
  33.3 17.5 %copy-start.1 = (bf16[4,2,8,128,128]{4,3,2,1,0:T(8,128)(2,1)S(1)}, bf16[4,2,8,128,128]{4,3,2,1,0:T(8,128)(2,1)}, u32[]{:S(2)}) copy-start(bf16[4,2,8,128,128]{4,3,2,1,0:T(8,128)(2,1)} %get-tuple-element.12.qd_hbm) | copy-start | bytes 6291460
  43.7 0.6 copy-start.5
  44.3 0.6 copy-start.8
  50.8 0.7 copy-start.6
  51.5 0.7 copy-start.7

commit v2 on v1

v2 whole, which is shorter than its diff:
```python
import math

import jax
import jax.numpy as jnp
from jax import lax
from jax.experimental import pallas as pl
from jax.experimental.pallas import tpu as pltpu
from jax.sharding import PartitionSpec as P

HEADS = 8
D = 128
B = 128
RING = 4
QUARTERS = 4
PART = 2
COLS = PART * B
LOCAL_ROWS = 16
LOCAL_KEYS = 32
ENTRIES = 64
GROUP = 8
TASKS = 272
FIRST_KEY = 64
SCALE = 1.0 / math.sqrt(D)
LOG2E = math.log2(math.e)
C2 = SCALE * LOG2E
NEG = -1e30
MASKED = -2e30
MESH = pl.DeviceIdType.MESH
ANY = pl.BlockSpec(memory_space=pl.ANY)
HBM = pl.BlockSpec(memory_space=pltpu.HBM)
VMEM = pl.BlockSpec(memory_space=pltpu.VMEM)
SMEM = pl.BlockSpec(memory_space=pltpu.SMEM)
BF = jnp.bfloat16
F32 = jnp.float32


class Place:
    def __init__(self):
        self.h = lax.axis_index("head")
        inner, outer = lax.axis_index("inner"), lax.axis_index("outer")
        self.x, self.z = lax.rem(outer, 4), lax.rem(inner, 4)
        self.y = (inner // 4) * 2 + outer // 4

    def device(self, x=None, y=None, z=None, h=None):
        x, y, z, h = (
            own if new is None else new
            for own, new in ((self.x, x), (self.y, y), (self.z, z), (self.h, h))
        )
        return (h, (y // 2) * 4 + z, lax.rem(y, 2) * 4 + x)

    def along(self, axis, step):
        at = lax.rem(getattr(self, axis) + step + RING, RING)
        return self.device(**{axis: at})

    def partner(self):
        return self.device(h=1 - self.h)

    def quarter(self, r):
        b, a = lax.rem(self.y, 2), lax.rem(self.x, 2)
        b, a = (1 - b if r & 2 else b), (1 - a if r & 1 else a)
        return 2 * b + a

    def square(self, r):
        b, a = lax.rem(self.y, 2), lax.rem(self.x, 2)
        y = self.y + 1 - 2 * b if r & 2 else self.y
        x = self.x + 1 - 2 * a if r & 1 else self.x
        return self.device(x=x, y=y)

    def around(self):
        near = [self.along(a, s) for a in ("x", "y", "z") for s in (1, -1)]
        return near + [self.partner(), self.square(3)]


def ring_at(me, step):
    return lax.rem(me + step + RING, RING)


def greet(devices):
    barrier = pltpu.get_barrier_semaphore()
    for device in devices:
        pl.semaphore_signal(barrier, inc=1, device_id=device, device_id_type=MESH)
    pl.semaphore_wait(barrier, len(devices))


class Gather:
    def __init__(self, place, axis, part, own, six, send, recv):
        self.me = getattr(place, axis)
        self.to = (place.along(axis, 1), place.along(axis, -1))
        self.part, self.own, self.six, self.send, self.recv = part, own, six, send, recv

    def copy(self, src, dst, way, k):
        return pltpu.make_async_remote_copy(
            src_ref=src,
            dst_ref=dst,
            send_sem=self.send,
            recv_sem=self.recv.at[way * 3 + k],
            device_id=self.to[way],
            device_id_type=MESH,
        )

    def start(self):
        for k in range(2):
            for way in range(2):
                for src, dst in self.own(k ^ way):
                    self.copy(src, dst, way, k).start()

    def whole(self, at, half, way, k):
        ref = self.part(at, half)
        return self.copy(ref, ref, way, k)

    def arrived(self, way, k):
        step = (-1 if way == 0 else 1) * (2 if k == 2 else 1)
        half = way if k == 2 else k ^ way
        self.whole(ring_at(self.me, step), half, way, k).wait_recv()

    def forward(self):
        for way in range(2):
            self.arrived(way, 0)
            step = -1 if way == 0 else 1
            self.whole(ring_at(self.me, step), way, way, 2).start()

    def finish(self):
        for way in range(2):
            self.arrived(way, 1)
        for way in range(2):
            self.arrived(way, 2)

    def sent(self):
        self.copy(self.six, self.six, 0, 0).wait_send()


def key_slot(place, j):
    n, a, b = j // 16, lax.rem(j // 4, 4), lax.rem(j, 4)
    owner = jnp.where(n == 0, place.h, 1 - place.h)
    yy, xx = jnp.where(n == 0, a, b), jnp.where(n == 0, b, a)
    return owner * 64 + (yy // 2) * 32 + place.z * 8 + lax.rem(yy, 2) * 4 + xx


def row_slot(place, i):
    zz, b, a = i // 4, lax.rem(i // 2, 2), lax.rem(i, 2)
    return (place.y // 2) * 32 + zz * 8 + b * 4 + (place.x // 2) * 2 + a


def tile_lists(place, qb_ref, kb_ref, kept):
    lanes = lax.broadcasted_iota(jnp.int32, (1, 128), 1)
    subs = lax.broadcasted_iota(jnp.int32, (LOCAL_ROWS, 1), 0)

    def key_step(j, row):
        return jnp.where(lanes == j, kb_ref[key_slot(place, j)], row)

    def row_step(i, column):
        return jnp.where(subs == i, qb_ref[row_slot(place, i)], column)

    key_pos = lax.fori_loop(0, LOCAL_KEYS, key_step, jnp.full((1, 128), -7, jnp.int32))
    row_pos = lax.fori_loop(0, LOCAL_ROWS, row_step, jnp.zeros((LOCAL_ROWS, 1), jnp.int32))
    wide = lax.broadcasted_iota(jnp.int32, (64, 128), 1)
    listed = jnp.zeros((64, 128), F32)
    for e in range(ENTRIES):
        listed = jnp.where(kept[:, e : e + 1] == wide, 1.0, listed)
    rows_of = (row_pos == lax.broadcasted_iota(jnp.int32, (LOCAL_ROWS, 64), 1)).astype(F32)
    keys_of = (key_pos == lax.broadcasted_iota(jnp.int32, (128, 128), 0)).astype(F32)
    mine = jnp.dot(
        jnp.dot(rows_of.astype(BF), listed.astype(BF), preferred_element_type=F32).astype(BF),
        keys_of.astype(BF),
        preferred_element_type=F32,
    )
    lane16 = lax.broadcasted_iota(jnp.int32, (LOCAL_ROWS, 128), 1)
    weight = lax.shift_left(jnp.ones_like(lane16), lax.rem(lane16, 16)).astype(F32)
    low = jnp.sum(jnp.where(lane16 < 16, mine * weight, 0.0), axis=1, keepdims=True)
    high = jnp.sum(
        jnp.where((lane16 >= 16) & (lane16 < 32), mine * weight, 0.0), axis=1, keepdims=True
    )
    bits = low.astype(jnp.int32) + lax.shift_left(
        high.astype(jnp.int32), jnp.full((LOCAL_ROWS, 1), 16, jnp.int32)
    )
    on = (key_pos == row_pos + FIRST_KEY).astype(F32)
    diagonal = jnp.sum(on * (lane16 - 99).astype(F32), axis=1, keepdims=True) + 99.0
    return jnp.where(lane16 == 0, bits, diagonal.astype(jnp.int32))


def gather_kernel(
    qb_hbm, kb_hbm, kept_hbm, q_ref, k_ref, v_ref, o_ref, g_ref,
    rows_out, keys_out, delta_ref, meta_ref,
    qb, kb, kept, o_vmem, g_vmem, parts,
    load, local, swap_send, swap_recv, s_send, s_recv, d_send, d_recv, zs, zr, cs, cr,
):
    place = Place()
    h, x, y, z = place.h, place.x, place.y, place.z
    pairs = ((o_ref, o_vmem), (g_ref, g_vmem), (kept_hbm, kept), (qb_hbm, qb), (kb_hbm, kb))
    loads = [pltpu.make_async_copy(src, dst, load.at[n]) for n, (src, dst) in enumerate(pairs)]
    for copy in loads:
        copy.start()
    greet(place.around())
    ours = pl.ds(pl.multiple_of(h * D, D), D)
    theirs = pl.ds(pl.multiple_of((1 - h) * D, D), D)

    swaps = [
        pltpu.make_async_remote_copy(
            src_ref=source.at[:, theirs],
            dst_ref=keys_out.at[1, x, y, n],
            send_sem=swap_send.at[n],
            recv_sem=swap_recv.at[n],
            device_id=place.partner(),
            device_id_type=MESH,
        )
        for n, source in enumerate((k_ref, v_ref))
    ]
    for copy in swaps:
        copy.start()

    def head(half, quarter, k):
        source = (q_ref, g_ref)[half]
        return source.at[:, pl.ds(pl.multiple_of((quarter * PART + k) * D, D), D)]

    def rows_copies(half):
        mine = place.quarter(0)
        return [(head(half, mine, k), rows_out.at[z, mine, half, k]) for k in range(PART)]

    def row_ring(r):
        part = lambda at, half: rows_out.at[at, place.quarter(r), half]
        own = rows_copies if r == 0 else lambda half: [(part(z, half),) * 2]
        return Gather(place, "z", part, own, rows_out.at[0, 0:3], zs.at[r], zr.at[r])

    gz = [row_ring(r) for r in range(QUARTERS)]

    def row_swaps(r):
        return [
            pltpu.make_async_remote_copy(
                src_ref=head(half, place.quarter(r), k),
                dst_ref=rows_out.at[z, place.quarter(0), half, k],
                send_sem=s_send.at[r],
                recv_sem=s_recv.at[r],
                device_id=place.square(r),
                device_id_type=MESH,
            )
            for half in range(2)
            for k in range(PART)
        ]

    def swapped(r):
        ref = rows_out.at[z, place.quarter(r)]
        return pltpu.make_async_remote_copy(
            src_ref=ref,
            dst_ref=ref,
            send_sem=s_send.at[r],
            recv_sem=s_recv.at[r],
            device_id=place.square(r),
            device_id_type=MESH,
        )

    def pass_rows(r):
        swapped(r).wait_recv()
        gz[r].start()

    def line(n):
        at_line = y if n == 0 else x
        part = lambda at, half: keys_out.at[n, at_line, at, half]
        if n == 0:
            own = lambda half: [((k_ref, v_ref)[half].at[:, ours], part(x, half))]
        else:
            own = lambda half: [(part(y, half),) * 2]
        return Gather(place, "xy"[n], part, own, keys_out.at[n, 0, 0:3], cs.at[n, 0], cr.at[n, 0])

    def cross(n, step):
        at_line, spot = (y, x) if n == 0 else (x, y)
        spot = ring_at(spot, step)
        part = lambda at, half: keys_out.at[n, at, spot, half]
        if n == 0 and step == 0:
            own = lambda half: [((k_ref, v_ref)[half].at[:, ours], part(y, half))]
        else:
            own = lambda half: [(part(at_line, half),) * 2]
        k = 1 + step % RING
        return Gather(place, "yx"[n], part, own, keys_out.at[n, 0, 0:3], cs.at[n, k], cr.at[n, k])

    lines = [line(n) for n in range(2)]
    crosses = [[cross(n, step) for step in (0, -1, 1, 2)] for n in range(2)]

    gz[0].start()
    for r in (2, 1):
        for copy in row_swaps(r):
            copy.start()
    lines[0].start()
    crosses[0][0].start()
    for copy in row_swaps(3):
        copy.start()
    for src, dst in rows_copies(0) + rows_copies(1):
        pltpu.make_async_copy(src, dst, local.at[0]).start()
    for n, source in enumerate((k_ref, v_ref)):
        pltpu.make_async_copy(source.at[:, ours], keys_out.at[0, y, x, n], local.at[1]).start()
    for copy in swaps:
        copy.wait_recv()
    lines[1].start()
    crosses[1][0].start()

    for copy in loads:
        copy.wait()
    for quarter in range(QUARTERS):
        for k in range(PART):
            cols = slice((quarter * PART + k) * D, (quarter * PART + k + 1) * D)
            product = g_vmem[:, cols].astype(F32) * o_vmem[:, cols].astype(F32)
            parts[quarter, :, k * B : (k + 1) * B] = jnp.sum(
                jnp.transpose(product), axis=0, keepdims=True
            )

    def delta_copy(r):
        return pltpu.make_async_remote_copy(
            src_ref=parts.at[place.quarter(r)],
            dst_ref=delta_ref.at[place.quarter(0)],
            send_sem=d_send.at[r],
            recv_sem=d_recv.at[r],
            device_id=place.square(r),
            device_id_type=MESH,
        )

    for r in (1, 2, 3):
        delta_copy(r).start()
    delta_ref[place.quarter(0)] = parts[place.quarter(0)]
    pass_rows(2)
    pass_rows(1)
    gz[0].forward()
    for n in range(2):
        lines[n].forward()
    for n in range(2):
        lines[n].arrived(0, 1)
        crosses[n][1].start()
        lines[n].arrived(1, 1)
        crosses[n][2].start()
    pass_rows(3)
    for n in range(2):
        crosses[n][0].forward()
    for n in range(2):
        lines[n].arrived(0, 2)
        lines[n].arrived(1, 2)
        crosses[n][3].start()
    gz[2].forward()
    gz[1].forward()
    for n in range(2):
        crosses[n][1].forward()
        crosses[n][2].forward()
    gz[3].forward()
    for n in range(2):
        crosses[n][3].forward()

    meta_ref[...] = tile_lists(place, qb, kb, kept)

    for n in range(2):
        for ring in crosses[n]:
            ring.finish()
    for ring in gz:
        ring.finish()
    for n, ref in enumerate((rows_out.at[z, place.quarter(0)], keys_out.at[0, y, x])):
        pltpu.make_async_copy(ref, ref, local.at[n]).wait()
    for copy in swaps:
        copy.wait_send()
    for r in (1, 2, 3):
        swapped(r).wait_send()
        delta_copy(r).wait_send()
        ref = delta_ref.at[place.quarter(r)]
        pltpu.make_async_remote_copy(
            src_ref=ref,
            dst_ref=ref,
            send_sem=d_send.at[r],
            recv_sem=d_recv.at[r],
            device_id=place.square(r),
            device_id_type=MESH,
        ).wait_recv()
    for ring in gz + lines + crosses[0] + crosses[1]:
        ring.sent()


def in_hbm(*arrays):
    return [pltpu.with_memory_space_constraint(a, pltpu.HBM) for a in arrays]


def gather(qb, kb, kept, q, k, v, o, g):
    return pl.pallas_call(
        gather_kernel,
        out_shape=(
            pltpu.VMEM((RING, QUARTERS, 2, PART, B, D), BF),
            pltpu.VMEM((2, RING, RING, 2, B, D), BF),
            pltpu.VMEM((QUARTERS, 1, COLS), F32),
            pltpu.VMEM((LOCAL_ROWS, 128), jnp.int32),
        ),
        in_specs=[HBM] * 8,
        out_specs=(ANY, ANY, VMEM, VMEM),
        scratch_shapes=[
            pltpu.SMEM((64,), jnp.int32),
            pltpu.SMEM((128,), jnp.int32),
            pltpu.VMEM((64, 64), jnp.int32),
            pltpu.VMEM((B, HEADS * D), BF),
            pltpu.VMEM((B, HEADS * D), BF),
            pltpu.VMEM((QUARTERS, 1, COLS), F32),
            pltpu.SemaphoreType.DMA((5,)),
            pltpu.SemaphoreType.DMA((2,)),
            pltpu.SemaphoreType.DMA((2,)),
            pltpu.SemaphoreType.DMA((2,)),
            pltpu.SemaphoreType.DMA((QUARTERS,)),
            pltpu.SemaphoreType.DMA((QUARTERS,)),
            pltpu.SemaphoreType.DMA((QUARTERS,)),
            pltpu.SemaphoreType.DMA((QUARTERS,)),
            pltpu.SemaphoreType.DMA((QUARTERS,)),
            pltpu.SemaphoreType.DMA((QUARTERS, 6)),
            pltpu.SemaphoreType.DMA((2, 1 + RING)),
            pltpu.SemaphoreType.DMA((2, 1 + RING, 6)),
        ],
        compiler_params=pltpu.CompilerParams(
            collective_id=0, has_side_effects=True, vmem_limit_bytes=8 * 2**20
        ),
        name="gather",
    )(*in_hbm(qb, kb, kept, q, k, v, o, g))


def across(a, b):
    return lax.dot_general(a, b, (((1,), (1,)), ((), ())), preferred_element_type=F32)


def fill_bias(bias_ref):
    keys = lax.broadcasted_iota(jnp.int32, (B, COLS), 0)
    rows = lax.rem(lax.broadcasted_iota(jnp.int32, (B, COLS), 1), B)
    bias_ref[0] = jnp.full((B, COLS), MASKED, F32)
    bias_ref[1] = jnp.where(keys <= rows, 0.0, MASKED)
    bias_ref[2] = jnp.zeros((B, COLS), F32)


def pop(bits, diagonal):
    j = (31 - lax.clz(bits)) & 31
    kind = jnp.where(bits == 0, 0, jnp.where(j == diagonal, 1, 2))
    return j, bits & ~lax.shift_left(jnp.int32(1), j), kind


def list_tasks(meta_ref, task_ref):
    def row(i, count):
        diagonal = meta_ref[i, 1]

        def more(state):
            return state[0] != 0

        def step(state):
            bits, count = state
            j0, bits, kind0 = pop(bits, diagonal)
            j1, bits, kind1 = pop(bits, diagonal)
            task_ref[count] = i + j0 * 16 + j1 * 512 + kind0 * 16384 + kind1 * 65536
            return bits, count + 1

        return lax.while_loop(more, step, (meta_ref[i, 0], count))[1]

    count = lax.fori_loop(0, LOCAL_ROWS, row, jnp.int32(0))
    for n in range(GROUP - 1):
        task_ref[count + n] = 0
    task_ref[TASKS - 1] = (count + GROUP - 1) // GROUP


def read_task(task_ref, n):
    e = task_ref[n]
    return (
        e & 15,
        (e // 16) & 31,
        (e // 512) & 31,
        (e // 16384) & 3,
        (e // 65536) & 3,
    )


def stats_kernel(meta_ref, rows_ref, keys_ref, st_ref, task_ref, m_ref, l_ref, bias_ref):
    list_tasks(meta_ref, task_ref)
    fill_bias(bias_ref)
    m_ref[...] = jnp.full_like(m_ref, NEG)
    l_ref[...] = jnp.zeros_like(l_ref)

    def group(n, _):
        results = []
        for t in range(GROUP):
            i, j0, j1, kind0, kind1 = read_task(task_ref, GROUP * n + t)
            queries = rows_ref[i, 0].reshape(COLS, D)
            keys = jnp.concatenate([keys_ref[j0, 0], keys_ref[j1, 0]], axis=0)
            s = across(keys, queries) * C2
            s = jnp.concatenate([s[:B] + bias_ref[kind0], s[B:] + bias_ref[kind1]], axis=0)
            s = s.reshape(2 * B // 8, 8, COLS)
            m = jnp.max(s, axis=0)
            results.append((i, m, jnp.sum(jnp.exp2(s - m[None]), axis=0)))
        for i, m, l in results:
            old = m_ref[i]
            new = jnp.maximum(old, m)
            m_ref[i] = new
            l_ref[i] = l_ref[i] * jnp.exp2(old - new) + l * jnp.exp2(m - new)
        return 0

    lax.fori_loop(0, task_ref[TASKS - 1], group, 0)
    m8 = m_ref[...]
    m = jnp.max(m8, axis=1, keepdims=True)
    st_ref[0] = m
    st_ref[1] = jnp.sum(l_ref[...] * jnp.exp2(m8 - m), axis=1, keepdims=True)


def statistics(meta, rows, keys):
    return pl.pallas_call(
        stats_kernel,
        out_shape=(
            pltpu.VMEM((2, LOCAL_ROWS, 1, COLS), F32),
            jax.ShapeDtypeStruct((TASKS,), jnp.int32),
        ),
        in_specs=[SMEM, VMEM, VMEM],
        out_specs=(VMEM, SMEM),
        scratch_shapes=[
            pltpu.VMEM((LOCAL_ROWS, 8, COLS), F32),
            pltpu.VMEM((LOCAL_ROWS, 8, COLS), F32),
            pltpu.VMEM((3, B, COLS), F32),
        ],
        compiler_params=pltpu.CompilerParams(vmem_limit_bytes=24 * 2**20),
        name="statistics",
    )(meta, rows, keys)


def exchange_kernel(
    st_ref, delta_ref, total_ref, all_delta_ref, sts, st_send, st_recv
):
    place = Place()
    z = place.z
    greet([place.along("z", step) for step in (1, 2, 3)])

    def copies(step):
        to = place.along("z", step)
        pairs = ((st_ref, sts.at[step - 1]), (delta_ref, all_delta_ref.at[z]))
        for n, (src, dst) in enumerate(pairs):
            yield pltpu.make_async_remote_copy(
                src_ref=src,
                dst_ref=dst,
                send_sem=st_send.at[step - 1, n],
                recv_sem=st_recv.at[step - 1, n],
                device_id=to,
                device_id_type=MESH,
            )

    for step in (2, 1, 3):
        for copy in copies(step):
            copy.start()
    all_delta_ref[z] = delta_ref[...]
    for step in (1, 3, 2):
        st_copy, delta_copy = copies(step)
        st_copy.wait()
        delta_copy.wait_send()
        ref = all_delta_ref.at[ring_at(z, -step)]
        pltpu.make_async_remote_copy(
            src_ref=ref,
            dst_ref=ref,
            send_sem=st_send.at[step - 1, 1],
            recv_sem=st_recv.at[step - 1, 1],
            device_id=place.along("z", step),
            device_id_type=MESH,
        ).wait_recv()
    top = st_ref[0]
    for n in range(3):
        top = jnp.maximum(top, sts[n, 0])
    total = st_ref[1] * jnp.exp2(st_ref[0] - top)
    for n in range(3):
        total = total + sts[n, 1] * jnp.exp2(sts[n, 0] - top)
    total_ref[...] = top + jnp.log2(total)


def exchange(st, delta):
    return pl.pallas_call(
        exchange_kernel,
        out_shape=(
            pltpu.VMEM((LOCAL_ROWS, 1, COLS), F32),
            pltpu.VMEM((RING, QUARTERS, 1, COLS), F32),
        ),
        in_specs=[VMEM, VMEM],
        out_specs=(VMEM, VMEM),
        scratch_shapes=[
            pltpu.VMEM((3, 2, LOCAL_ROWS, 1, COLS), F32),
            pltpu.SemaphoreType.DMA((3, 2)),
            pltpu.SemaphoreType.DMA((3, 2)),
        ],
        compiler_params=pltpu.CompilerParams(
            collective_id=1, has_side_effects=True, vmem_limit_bytes=8 * 2**20
        ),
        name="exchange",
    )(st, delta)


def grads_kernel(
    task_ref, rows_ref, keys_ref, total_ref, delta_ref, dq_ref, dkv_ref,
    dq_acc, dk_acc, dv_acc, bias_ref, p_ref, ds_ref,
):
    fill_bias(bias_ref)
    dq_acc[...] = jnp.zeros_like(dq_acc)
    dk_acc[...] = jnp.zeros_like(dk_acc)
    dv_acc[...] = jnp.zeros_like(dv_acc)

    def group(n, _):
        tasks = [read_task(task_ref, GROUP * n + t) for t in range(GROUP)]
        for t, (i, j0, j1, kind0, kind1) in enumerate(tasks):
            keys = jnp.concatenate([keys_ref[j0, 0], keys_ref[j1, 0]], axis=0)
            values = jnp.concatenate([keys_ref[j0, 1], keys_ref[j1, 1]], axis=0)
            s = across(keys, rows_ref[i, 0].reshape(COLS, D)) * C2 - total_ref[i]
            s = jnp.concatenate([s[:B] + bias_ref[kind0], s[B:] + bias_ref[kind1]], axis=0)
            p = jnp.exp2(s)
            p_ref[t] = p.astype(BF)
            dp = across(values, rows_ref[i, 1].reshape(COLS, D))
            ds_ref[t] = (p * (dp - delta_ref[i])).astype(BF)
        for t, (i, j0, j1, _, _) in enumerate(tasks):
            keys = jnp.concatenate([keys_ref[j0, 0], keys_ref[j1, 0]], axis=0)
            ds = ds_ref[t]
            dv = jnp.dot(p_ref[t], rows_ref[i, 1].reshape(COLS, D), preferred_element_type=F32)
            dk = jnp.dot(ds, rows_ref[i, 0].reshape(COLS, D), preferred_element_type=F32)
            dq_acc[i] += jnp.dot(jnp.transpose(keys), ds, preferred_element_type=F32)
            dk_acc[j0] += dk[:B]
            dk_acc[j1] += dk[B:]
            dv_acc[j0] += dv[:B]
            dv_acc[j1] += dv[B:]
        return 0

    lax.fori_loop(0, task_ref[TASKS - 1], group, 0)

    def write(j, _):
        dkv_ref[j, 0] = (dk_acc[j] * SCALE).astype(BF)
        dkv_ref[j, 1] = dv_acc[j].astype(BF)
        return 0

    lax.fori_loop(0, LOCAL_KEYS, write, 0, unroll=8)

    def write_rows(i, _):
        for k in range(PART):
            dq_ref[i, k] = (dq_acc[i, :, k * B : (k + 1) * B] * SCALE).astype(BF)
        return 0

    lax.fori_loop(0, LOCAL_ROWS, write_rows, 0, unroll=8)


def grads(tasks, rows, keys, total, delta):
    return pl.pallas_call(
        grads_kernel,
        out_shape=(
            pltpu.VMEM((LOCAL_ROWS, PART, D, B), BF),
            pltpu.VMEM((LOCAL_KEYS, 2, B, D), BF),
        ),
        in_specs=[SMEM] + [VMEM] * 4,
        out_specs=(VMEM, VMEM),
        scratch_shapes=[
            pltpu.VMEM((LOCAL_ROWS, D, COLS), F32),
            pltpu.VMEM((LOCAL_KEYS, B, D), F32),
            pltpu.VMEM((LOCAL_KEYS, B, D), F32),
            pltpu.VMEM((3, B, COLS), F32),
            pltpu.VMEM((GROUP, 2 * B, COLS), BF),
            pltpu.VMEM((GROUP, 2 * B, COLS), BF),
        ],
        compiler_params=pltpu.CompilerParams(vmem_limit_bytes=32 * 2**20),
        name="grads",
    )(tasks, rows, keys, total, delta)


class Scatter:
    def __init__(self, place, axis, part, near, far, mid, six, send, recv):
        self.me = getattr(place, axis)
        self.to = (place.along(axis, 1), place.along(axis, -1))
        self.part, self.near, self.far, self.mid, self.six = part, near, far, mid, six
        self.send, self.recv = send, recv

    def copy(self, src, dst, way, k):
        return pltpu.make_async_remote_copy(
            src_ref=src,
            dst_ref=dst,
            send_sem=self.send,
            recv_sem=self.recv.at[way * 3 + k],
            device_id=self.to[way],
            device_id_type=MESH,
        )

    def far_copy(self, way):
        return self.copy(self.part(ring_at(self.me, 2), way), self.far.at[way], way, 0)

    def plain_copy(self, way):
        step = 1 if way == 0 else -1
        return self.copy(
            self.part(ring_at(self.me, step), 1 - way), self.near.at[way, 1 - way], way, 1
        )

    def mid_copy(self, way):
        return self.copy(self.mid.at[way], self.near.at[way, way], way, 2)

    def start_far(self):
        for way in range(2):
            self.far_copy(way).start()

    def start_plain(self, way):
        self.plain_copy(way).start()

    def forward(self):
        for way in range(2):
            step = 1 if way == 0 else -1
            self.far_copy(way).wait_recv()
            own = self.part(ring_at(self.me, step), way)[...].astype(F32)
            self.mid[way] = (self.far[way].astype(F32) + own).astype(BF)
            self.mid_copy(way).start()

    def finish(self):
        for way in range(2):
            self.plain_copy(way).wait_recv()
        for way in range(2):
            self.mid_copy(way).wait_recv()

    def total(self, half, own=None):
        own = self.part(self.me, half)[...].astype(F32) if own is None else own
        return own + self.near[0, half].astype(F32) + self.near[1, half].astype(F32)

    def sent(self):
        self.copy(self.six, self.six, 0, 0).wait_send()


STEPS = (2, -1, 1, 0)
MEMBERS = (3, 2, 1, 0)


def scatter_kernel(
    dq_ref, dkv_ref, qg_ref, kg_ref, vg_ref,
    zn, zf, zm, cn, cf, cm, ln, lf, lm, sums, own_sum, fin, qout,
    zs, zr, cs, cr, ls, lr, swap_send, swap_recv, q_send, q_recv, local,
):
    place = Place()
    h, x, y, z = place.h, place.x, place.y, place.z
    greet(place.around())

    def row_ring(k):
        number = place.quarter(MEMBERS[k])
        part = lambda at, half: dq_ref.at[at, number, half]
        return Scatter(place, "z", part, zn.at[k], zf.at[k], zm.at[k], dq_ref.at[0, 0:3], zs.at[k], zr.at[k])

    def cross(n, k):
        spot = ring_at((x, y)[n], STEPS[k])
        part = lambda at, half: dkv_ref.at[n, at, spot, half]
        return Scatter(
            place, "yx"[n], part, cn.at[n, k], cf.at[n, k], cm.at[n, k], dkv_ref.at[n, 0, 0:3],
            cs.at[n, k], cr.at[n, k],
        )

    def line(n):
        part = lambda at, half: sums.at[n, at, half]
        return Scatter(place, "xy"[n], part, ln.at[n], lf.at[n], lm.at[n], sums.at[n, 0:3], ls.at[n], lr.at[n])

    rows = [row_ring(k) for k in range(RING)]
    crosses = [[cross(n, k) for k in range(RING)] for n in range(2)]
    lines = [line(n) for n in range(2)]
    waves = [(crosses[0][k], crosses[1][k], rows[k]) for k in range(RING)]
    for wave in waves:
        for ring in wave:
            ring.start_far()
    for wave in waves:
        for ring in wave:
            for way in range(2):
                ring.start_plain(way)
    for wave in waves:
        for ring in wave:
            ring.forward()

    part_cols = pl.ds(pl.multiple_of(place.quarter(0) * COLS, COLS), COLS)

    def q_copy(k):
        r = MEMBERS[k]
        return pltpu.make_async_remote_copy(
            src_ref=qout.at[k],
            dst_ref=qg_ref.at[:, part_cols],
            send_sem=q_send.at[r],
            recv_sem=q_recv.at[r],
            device_id=place.square(r),
            device_id_type=MESH,
        )

    q_own = pltpu.make_async_copy(qout.at[RING - 1], qg_ref.at[:, part_cols], local.at[0])
    for k in range(RING):
        for n in range(2):
            ring = crosses[n][k]
            ring.finish()
            for half in range(2):
                total = ring.total(half)
                if STEPS[k] == 0:
                    own_sum[n, half] = total
                else:
                    sums[n, ring_at((x, y)[n], STEPS[k]), half] = total.astype(BF)
            if STEPS[k] == 2:
                lines[n].start_far()
            elif STEPS[k] != 0:
                lines[n].start_plain(0 if STEPS[k] == 1 else 1)
        if k == 2:
            for n in range(2):
                lines[n].forward()
        rows[k].finish()
        for half in range(PART):
            qout[k, :, half * D : (half + 1) * D] = jnp.transpose(rows[k].total(half)).astype(BF)
        if MEMBERS[k]:
            q_copy(k).start()
        else:
            q_own.start()

    ours = pl.ds(pl.multiple_of(h * D, D), D)
    theirs = pl.ds(pl.multiple_of((1 - h) * D, D), D)
    swaps = [
        pltpu.make_async_remote_copy(
            src_ref=fin.at[1, n],
            dst_ref=target.at[:, ours],
            send_sem=swap_send.at[n],
            recv_sem=swap_recv.at[n],
            device_id=place.partner(),
            device_id_type=MESH,
        )
        for n, target in enumerate((kg_ref, vg_ref))
    ]
    outs = [
        pltpu.make_async_copy(fin.at[0, n], target.at[:, ours], local.at[1 + n])
        for n, target in enumerate((kg_ref, vg_ref))
    ]
    for n, copies in ((1, swaps), (0, outs)):
        lines[n].finish()
        for half in range(2):
            fin[n, half] = lines[n].total(half, own_sum[n, half]).astype(BF)
        for copy in copies:
            copy.start()
    for copy in outs:
        copy.wait()
    q_own.wait()
    for n, target in enumerate((kg_ref, vg_ref)):
        swaps[n].wait_send()
        ref = target.at[:, theirs]
        pltpu.make_async_remote_copy(
            src_ref=ref,
            dst_ref=ref,
            send_sem=swap_send.at[n],
            recv_sem=swap_recv.at[n],
            device_id=place.partner(),
            device_id_type=MESH,
        ).wait_recv()
    for k in range(RING - 1):
        q_copy(k).wait_send()
        r = MEMBERS[k]
        ref = qg_ref.at[:, pl.ds(pl.multiple_of(place.quarter(r) * COLS, COLS), COLS)]
        pltpu.make_async_remote_copy(
            src_ref=ref,
            dst_ref=ref,
            send_sem=q_send.at[r],
            recv_sem=q_recv.at[r],
            device_id=place.square(r),
            device_id_type=MESH,
        ).wait_recv()
    for ring in rows + crosses[0] + crosses[1] + lines:
        ring.sent()


def scatter(dq, dkv):
    def ring_scratch(*rings):
        return [
            pltpu.VMEM(rings + (2, 2, B, D), BF),
            pltpu.VMEM(rings + (2, B, D), BF),
            pltpu.VMEM(rings + (2, B, D), BF),
        ]

    def ring_semaphores(*rings):
        return [pltpu.SemaphoreType.DMA(rings), pltpu.SemaphoreType.DMA(rings + (6,))]

    return pl.pallas_call(
        scatter_kernel,
        out_shape=(
            pltpu.VMEM((B, HEADS * D), BF),
            pltpu.VMEM((B, 2 * D), BF),
            pltpu.VMEM((B, 2 * D), BF),
        ),
        in_specs=[VMEM, VMEM],
        out_specs=(VMEM, VMEM, VMEM),
        scratch_shapes=ring_scratch(RING)
        + ring_scratch(2, RING)
        + ring_scratch(2)
        + [
            pltpu.VMEM((2, RING, 2, B, D), BF),
            pltpu.VMEM((2, 2, B, D), F32),
            pltpu.VMEM((2, 2, B, D), BF),
            pltpu.VMEM((QUARTERS, B, COLS), BF),
        ]
        + ring_semaphores(RING)
        + ring_semaphores(2, RING)
        + ring_semaphores(2)
        + [
            pltpu.SemaphoreType.DMA((2,)),
            pltpu.SemaphoreType.DMA((2,)),
            pltpu.SemaphoreType.DMA((QUARTERS,)),
            pltpu.SemaphoreType.DMA((QUARTERS,)),
            pltpu.SemaphoreType.DMA((3,)),
        ],
        compiler_params=pltpu.CompilerParams(
            collective_id=2, has_side_effects=True, vmem_limit_bytes=24 * 2**20
        ),
        name="scatter",
    )(dq.reshape(RING, QUARTERS, PART, D, B), dkv.reshape(2, RING, RING, 2, B, D))


def store_kernel(q_ref, k_ref, v_ref, qg_ref, kg_ref, vg_ref, sems):
    copies = [
        pltpu.make_async_copy(src, dst, sems.at[n])
        for n, (src, dst) in enumerate(((q_ref, qg_ref), (k_ref, kg_ref), (v_ref, vg_ref)))
    ]
    for copy in copies:
        copy.start()
    for copy in copies:
        copy.wait()


def store(*results):
    return pl.pallas_call(
        store_kernel,
        out_shape=tuple(pltpu.HBM(r.shape, r.dtype) for r in results),
        in_specs=[VMEM] * 3,
        out_specs=(HBM,) * 3,
        scratch_shapes=[pltpu.SemaphoreType.DMA((3,))],
        compiler_params=pltpu.CompilerParams(vmem_limit_bytes=4 * 2**20),
        name="store",
    )(*results)


def body(q, k, v, o, g, query_blocks, key_blocks, kept_blocks):
    rows, keys, delta, meta = gather(query_blocks, key_blocks, kept_blocks, q, k, v, o, g)
    rows = rows.reshape(LOCAL_ROWS, 2, PART, B, D)
    keys = keys.reshape(LOCAL_KEYS, 2, B, D)
    st, tasks = statistics(meta, rows, keys)
    total, all_delta = exchange(st, delta)
    dq, dkv = grads(tasks, rows, keys, total, all_delta.reshape(LOCAL_ROWS, 1, COLS))
    return store(*scatter(dq, dkv))


def solution(mesh):
    rows, stored = P(("inner", "outer"), "head"), P(("head", "inner", "outer"), None)
    return jax.shard_map(
        body,
        mesh=mesh,
        in_specs=(rows, stored, stored, rows, rows, P(), P(), P()),
        out_specs=(rows, stored, stored),
        check_vma=False,
    )
```

time: 92.4 us -> 69.6 us (0.75)
  Pallas kernels: 80.4 us -> 68.8 us
  local copies, waits for them, and re-layouts: 10.8 us -> 0 us
    pallas_call x5 -> x6, Pallas kernels: 80.4 us -> 68.8 us  [the longest x1 30 us: scatter(): pl.pallas_call(scatter_kernel, out_shape=(pltpu.VMEM((B, HEADS * D), BF),...]
    unnamed x25 -> x0, local copies, waits for them, and re-layouts: 10.8 us -> none
where the time goes in v2:
time: 69.6 us; the launch traced here: 69.5 us
  Pallas kernels  68.8 us (99%)
    pallas_call x1, Pallas kernels, scatter(): pl.pallas_call(scatter_kernel, out_shape=(pltpu.VMEM((B, HEADS * D), BF),...  30 us
    pallas_call x1, Pallas kernels, gather(): pl.pallas_call(gather_kernel, out_shape=(pltpu.VMEM((RING, QUARTERS, 2, P...  26 us
    pallas_call x1, Pallas kernels, exchange(): pl.pallas_call(exchange_kernel, out_shape=(pltpu.VMEM((LOCAL_ROWS, 1, COL...  4.72 us
    pallas_call x1, Pallas kernels, grads(): pl.pallas_call(grads_kernel, out_shape=(pltpu.VMEM((LOCAL_ROWS, PART, D,...  4.3 us
    pallas_call x1, Pallas kernels, statistics(): pl.pallas_call(stats_kernel, out_shape=(pltpu.VMEM((2, LOCAL_ROWS, 1, COL...  3.08 us

profile of v2, /device:TPU:1, one launch (start us, length us, event | category | flops | bytes accessed | tf_op | source)
XLA Modules:
  0.0 69.5 jit_solution(16418514885591189609)
XLA Ops:
  0.6 26.0 %gather.1 = (bf16[4,4,2,2,128,128]{5,4,3,2,1,0:T(8,128)(2,1)S(1)}, bf16[2,4,4,2,128,128]{5,4,3,2,1,0:T(8,128)(2,1)S(1)}, f32[4,1,256]{2,1,0:T(1,128)S(1)}, s32[16,128]{1,0:T(8,128)S(1)}) custom-call(s32[64]{0:T(128)} %qb_hbm.1, s32[128]{0:T(128)} %kb_hbm.1, s32[64,64]{1,0:T(8,128)} %kept_hbm.1, bf16[128,1024]{1,0:T(8,128)(2,1)} %q_ref.1, ...), custom_call_target="tpu_custom_call" | custom-call | tf_op jit(solution)/shard_map/gather/pallas_call | solution.py:376
  26.6 3.1 %statistics.1 = (f32[2,16,1,256]{3,2,1,0:T(1,128)S(1)}, s32[272]{0:T(512)S(1)}) custom-call(s32[16,128]{1,0:T(8,128)S(1)} %get-tuple-element.16.meta_ref, bf16[16,2,2,128,128]{4,3,2,1,0:T(8,128)(2,1)S(1)} %bitcast.5, bf16[32,2,128,128]{3,2,1,0:T(8,128)(2,1)S(1)} %bitcast.7), custom_call_target="tpu_custom_call" | custom-call | tf_op jit(solution)/shard_map/statistics/pallas_call | solution.py:496
  29.7 4.7 %exchange.1 = (f32[16,1,256]{2,1,0:T(1,128)S(1)}, f32[4,4,1,256]{3,2,1,0:T(1,128)S(1)}) custom-call(f32[2,16,1,256]{3,2,1,0:T(1,128)S(1)} %get-tuple-element.20.st_ref, f32[4,1,256]{2,1,0:T(1,128)S(1)} %get-tuple-element.21.delta_ref), custom_call_target="tpu_custom_call" | custom-call | tf_op jit(solution)/shard_map/exchange/pallas_call | solution.py:561
  34.4 4.3 %grads.1 = (bf16[16,2,128,128]{3,2,1,0:T(8,128)(2,1)S(1)}, bf16[32,2,128,128]{3,2,1,0:T(8,128)(2,1)S(1)}) custom-call(s32[272]{0:T(512)S(1)} %get-tuple-element.19.task_ref, bf16[16,2,2,128,128]{4,3,2,1,0:T(8,128)(2,1)S(1)} %bitcast.6, bf16[32,2,128,128]{3,2,1,0:T(8,128)(2,1)S(1)} %bitcast.8, f32[16,1,256]{2,1,0:T(1,128)S(1)} %get-tuple-element.22.total_ref, ...), custom_call_target="tpu_custom_call" | custom-call | tf_op jit(solution)/shard_map/grads/pallas_call | solution.py:631
  38.7 30.0 %scatter.1 = (bf16[128,1024]{1,0:T(8,128)(2,1)S(1)}, bf16[128,256]{1,0:T(8,128)(2,1)S(1)}, bf16[128,256]{1,0:T(8,128)(2,1)S(1)}) custom-call(bf16[4,4,2,128,128]{4,3,2,1,0:T(8,128)(2,1)S(1)} %bitcast.10, bf16[2,4,4,2,128,128]{5,4,3,2,1,0:T(8,128)(2,1)S(1)} %bitcast.9), custom_call_target="tpu_custom_call" | custom-call | tf_op jit(solution)/shard_map/scatter/pallas_call | solution.py:858
  68.7 0.8 %store.1 = (bf16[128,1024]{1,0:T(8,128)(2,1)}, bf16[128,256]{1,0:T(8,128)(2,1)}, bf16[128,256]{1,0:T(8,128)(2,1)}) custom-call(bf16[128,1024]{1,0:T(8,128)(2,1)S(1)} %get-tuple-element.26.q_ref, bf16[128,256]{1,0:T(8,128)(2,1)S(1)} %get-tuple-element.27.k_ref, bf16[128,256]{1,0:T(8,128)(2,1)S(1)} %get-tuple-element.28.v_ref), custom_call_target="tpu_custom_call" | custom-call | tf_op jit(solution)/shard_map/store/pallas_call | solution.py:905

commit v3 on v2

--- a/solution.py
+++ b/solution.py
@@ -19,6 +19,7 @@
 ENTRIES = 64
 GROUP = 8
 TASKS = 272
+EARLY = 120
 FIRST_KEY = 64
 SCALE = 1.0 / math.sqrt(D)
 LOG2E = math.log2(math.e)
@@ -175,14 +176,60 @@
     )
     on = (key_pos == row_pos + FIRST_KEY).astype(F32)
     diagonal = jnp.sum(on * (lane16 - 99).astype(F32), axis=1, keepdims=True) + 99.0
-    return jnp.where(lane16 == 0, bits, diagonal.astype(jnp.int32))
+    meta = jnp.where(lane16 == 0, bits, diagonal.astype(jnp.int32))
+    return meta, mine, diagonal
+
+
+def halves_up(count):
+    return lax.shift_right_logical(
+        count.astype(jnp.int32) + 1, jnp.ones(count.shape, jnp.int32)
+    ).astype(F32)
+
+
+def exact(a, b, dims=(((1,), (0,)), ((), ()))):
+    return lax.dot_general(a.astype(BF), b.astype(BF), dims, preferred_element_type=F32)
+
+
+def early_tasks(mine, diagonal):
+    sub = lax.broadcasted_iota(jnp.int32, (LOCAL_ROWS, 128), 0)
+    lane = lax.broadcasted_iota(jnp.int32, (LOCAL_ROWS, 128), 1)
+    count = jnp.broadcast_to(jnp.sum(mine, axis=1, keepdims=True), (LOCAL_ROWS, 128))
+    tasks = halves_up(count)
+    before = (
+        lax.broadcasted_iota(jnp.int32, (LOCAL_ROWS, LOCAL_ROWS), 1)
+        < lax.broadcasted_iota(jnp.int32, (LOCAL_ROWS, LOCAL_ROWS), 0)
+    ).astype(F32)
+    start = exact(before, tasks)
+    at = lane.astype(F32)
+    chosen = ((start <= at) & (at < start + tasks)).astype(F32)
+
+    def of_row(column):
+        return jnp.sum(chosen * column, axis=0, keepdims=True)
+
+    row, first, diag = of_row(sub.astype(F32)), of_row(start), of_row(diagonal)
+    lower = (
+        lax.broadcasted_iota(jnp.int32, (128, 128), 0)
+        < lax.broadcasted_iota(jnp.int32, (128, 128), 1)
+    ).astype(F32)
+    rank = exact(mine, lower)
+    down = (((0,), (0,)), ((), ()))
+    mine_t, rank_t = exact(mine, chosen, down), exact(rank, chosen, down)
+    block = lax.broadcasted_iota(jnp.int32, (128, 128), 0).astype(F32)
+    code = row
+    for k in range(2):
+        here = mine_t * (rank_t == 2.0 * (at[:1] - first) + k).astype(F32)
+        j = jnp.sum(here * block, axis=0, keepdims=True)
+        valid = jnp.sum(here, axis=0, keepdims=True)
+        kind = valid * jnp.where(j == diag, 1.0, 2.0)
+        code = code + j * (16.0, 512.0)[k] + kind * (16384.0, 65536.0)[k]
+    return code, jnp.sum(tasks, axis=0, keepdims=True)
 
 
 def gather_kernel(
     qb_hbm, kb_hbm, kept_hbm, q_ref, k_ref, v_ref, o_ref, g_ref,
-    rows_out, keys_out, delta_ref, meta_ref,
+    rows_out, keys_out, delta_ref, meta_ref, list_ref,
     qb, kb, kept, o_vmem, g_vmem, parts,
-    load, local, swap_send, swap_recv, s_send, s_recv, d_send, d_recv, zs, zr, cs, cr,
+    load, local, swap_send, swap_recv, s_send, s_recv, d_send, d_recv, dz_send, dz_recv, zs, zr, cs, cr,
 ):
     place = Place()
     h, x, y, z = place.h, place.x, place.y, place.z
@@ -190,7 +237,7 @@
     loads = [pltpu.make_async_copy(src, dst, load.at[n]) for n, (src, dst) in enumerate(pairs)]
     for copy in loads:
         copy.start()
-    greet(place.around())
+    greet(place.around() + [place.along("z", 2)])
     ours = pl.ds(pl.multiple_of(h * D, D), D)
     theirs = pl.ds(pl.multiple_of((1 - h) * D, D), D)
 
@@ -275,22 +322,35 @@
     lines = [line(n) for n in range(2)]
     crosses = [[cross(n, step) for step in (0, -1, 1, 2)] for n in range(2)]
 
-    gz[0].start()
-    for r in (2, 1):
+    def send_rows(r):
         for copy in row_swaps(r):
             copy.start()
-    lines[0].start()
-    crosses[0][0].start()
-    for copy in row_swaps(3):
-        copy.start()
+
+    def start_cross(n, way):
+        lines[n].arrived(way, 1)
+        crosses[n][1 + way].start()
+
+    def start_far(n):
+        for way in range(2):
+            lines[n].arrived(way, 2)
+        crosses[n][3].start()
+
+    def start_keys(n):
+        lines[n].start()
+        crosses[n][0].start()
+
+    gz[0].start()
+    send_rows(2)
+    send_rows(1)
+    start_keys(0)
+    send_rows(3)
     for src, dst in rows_copies(0) + rows_copies(1):
         pltpu.make_async_copy(src, dst, local.at[0]).start()
     for n, source in enumerate((k_ref, v_ref)):
         pltpu.make_async_copy(source.at[:, ours], keys_out.at[0, y, x, n], local.at[1]).start()
     for copy in swaps:
         copy.wait_recv()
-    lines[1].start()
-    crosses[1][0].start()
+    start_keys(1)
 
     for copy in loads:
         copy.wait()
@@ -305,33 +365,58 @@
     def delta_copy(r):
         return pltpu.make_async_remote_copy(
             src_ref=parts.at[place.quarter(r)],
-            dst_ref=delta_ref.at[place.quarter(0)],
+            dst_ref=delta_ref.at[z, place.quarter(0)],
             send_sem=d_send.at[r],
             recv_sem=d_recv.at[r],
             device_id=place.square(r),
             device_id_type=MESH,
         )
 
+    def swapped_delta(r):
+        ref = delta_ref.at[z, place.quarter(r)]
+        return pltpu.make_async_remote_copy(
+            src_ref=ref,
+            dst_ref=ref,
+            send_sem=d_send.at[r],
+            recv_sem=d_recv.at[r],
+            device_id=place.square(r),
+            device_id_type=MESH,
+        )
+
+    def delta_line(step, at):
+        return pltpu.make_async_remote_copy(
+            src_ref=delta_ref.at[at],
+            dst_ref=delta_ref.at[at],
+            send_sem=dz_send.at[step - 1],
+            recv_sem=dz_recv.at[step - 1],
+            device_id=place.along("z", step),
+            device_id_type=MESH,
+        )
+
     for r in (1, 2, 3):
         delta_copy(r).start()
-    delta_ref[place.quarter(0)] = parts[place.quarter(0)]
+    delta_ref[z, place.quarter(0)] = parts[place.quarter(0)]
     pass_rows(2)
     pass_rows(1)
     gz[0].forward()
-    for n in range(2):
-        lines[n].forward()
-    for n in range(2):
-        lines[n].arrived(0, 1)
-        crosses[n][1].start()
-        lines[n].arrived(1, 1)
-        crosses[n][2].start()
+    lines[0].forward()
+    start_cross(0, 0)
+    start_cross(0, 1)
+
+    meta, mine, diagonal = tile_lists(place, qb, kb, kept)
+    meta_ref[...] = meta
+    code, count = early_tasks(mine, diagonal)
+    sub = lax.broadcasted_iota(jnp.int32, (8, 128), 0)
+    list_ref[...] = jnp.where(sub == 0, code, count).astype(jnp.int32)
+
+    lines[1].forward()
+    start_cross(1, 0)
+    start_cross(1, 1)
     pass_rows(3)
     for n in range(2):
         crosses[n][0].forward()
     for n in range(2):
-        lines[n].arrived(0, 2)
-        lines[n].arrived(1, 2)
-        crosses[n][3].start()
+        start_far(n)
     gz[2].forward()
     gz[1].forward()
     for n in range(2):
@@ -340,8 +425,10 @@
     gz[3].forward()
     for n in range(2):
         crosses[n][3].forward()
-
-    meta_ref[...] = tile_lists(place, qb, kb, kept)
+    for r in (1, 2, 3):
+        swapped_delta(r).wait_recv()
+    for step in (1, 2, 3):
+        delta_line(step, z).start()
 
     for n in range(2):
         for ring in crosses[n]:
@@ -354,16 +441,10 @@
         copy.wait_send()
     for r in (1, 2, 3):
         swapped(r).wait_send()
-        delta_copy(r).wait_send()
-        ref = delta_ref.at[place.quarter(r)]
-        pltpu.make_async_remote_copy(
-            src_ref=ref,
-            dst_ref=ref,
-            send_sem=d_send.at[r],
-            recv_sem=d_recv.at[r],
-            device_id=place.square(r),
-            device_id_type=MESH,
-        ).wait_recv()
+        swapped_delta(r).wait_send()
+    for step in (1, 2, 3):
+        delta_line(step, z).wait_send()
+        delta_line(step, ring_at(z, -step)).wait_recv()
     for ring in gz + lines + crosses[0] + crosses[1]:
         ring.sent()
 
@@ -378,11 +459,12 @@
         out_shape=(
             pltpu.VMEM((RING, QUARTERS, 2, PART, B, D), BF),
             pltpu.VMEM((2, RING, RING, 2, B, D), BF),
-            pltpu.VMEM((QUARTERS, 1, COLS), F32),
+            pltpu.VMEM((RING, QUARTERS, 1, COLS), F32),
             pltpu.VMEM((LOCAL_ROWS, 128), jnp.int32),
+            pltpu.VMEM((8, 128), jnp.int32),
         ),
         in_specs=[HBM] * 8,
-        out_specs=(ANY, ANY, VMEM, VMEM),
+        out_specs=(ANY, ANY, VMEM, VMEM, VMEM),
         scratch_shapes=[
             pltpu.SMEM((64,), jnp.int32),
             pltpu.SMEM((128,), jnp.int32),
@@ -398,6 +480,8 @@
             pltpu.SemaphoreType.DMA((QUARTERS,)),
             pltpu.SemaphoreType.DMA((QUARTERS,)),
             pltpu.SemaphoreType.DMA((QUARTERS,)),
+            pltpu.SemaphoreType.DMA((3,)),
+            pltpu.SemaphoreType.DMA((3,)),
             pltpu.SemaphoreType.DMA((QUARTERS,)),
             pltpu.SemaphoreType.DMA((QUARTERS, 6)),
             pltpu.SemaphoreType.DMA((2, 1 + RING)),
@@ -461,8 +545,22 @@
     )
 
 
-def stats_kernel(meta_ref, rows_ref, keys_ref, st_ref, task_ref, m_ref, l_ref, bias_ref):
-    list_tasks(meta_ref, task_ref)
+def take_tasks(meta_ref, list_ref, task_ref):
+    count = list_ref[1, 0]
+
+    @pl.when(count <= EARLY)
+    def _():
+        for n in range(EARLY):
+            task_ref[n] = list_ref[0, n]
+        task_ref[TASKS - 1] = (count + GROUP - 1) // GROUP
+
+    @pl.when(count > EARLY)
+    def _():
+        list_tasks(meta_ref, task_ref)
+
+
+def stats_kernel(meta_ref, list_ref, rows_ref, keys_ref, st_ref, task_ref, m_ref, l_ref, bias_ref):
+    take_tasks(meta_ref, list_ref, task_ref)
     fill_bias(bias_ref)
     m_ref[...] = jnp.full_like(m_ref, NEG)
     l_ref[...] = jnp.zeros_like(l_ref)
@@ -492,96 +590,77 @@
     st_ref[1] = jnp.sum(l_ref[...] * jnp.exp2(m8 - m), axis=1, keepdims=True)
 
 
-def statistics(meta, rows, keys):
+def statistics(meta, lists, rows, keys):
     return pl.pallas_call(
         stats_kernel,
-        out_shape=(
-            pltpu.VMEM((2, LOCAL_ROWS, 1, COLS), F32),
-            jax.ShapeDtypeStruct((TASKS,), jnp.int32),
-        ),
-        in_specs=[SMEM, VMEM, VMEM],
-        out_specs=(VMEM, SMEM),
+        out_shape=pltpu.VMEM((2, LOCAL_ROWS, 1, COLS), F32),
+        in_specs=[SMEM, SMEM, VMEM, VMEM],
+        out_specs=VMEM,
         scratch_shapes=[
+            pltpu.SMEM((TASKS,), jnp.int32),
             pltpu.VMEM((LOCAL_ROWS, 8, COLS), F32),
             pltpu.VMEM((LOCAL_ROWS, 8, COLS), F32),
             pltpu.VMEM((3, B, COLS), F32),
         ],
         compiler_params=pltpu.CompilerParams(vmem_limit_bytes=24 * 2**20),
         name="statistics",
-    )(meta, rows, keys)
-
-
-def exchange_kernel(
-    st_ref, delta_ref, total_ref, all_delta_ref, sts, st_send, st_recv
-):
-    place = Place()
-    z = place.z
-    greet([place.along("z", step) for step in (1, 2, 3)])
-
-    def copies(step):
-        to = place.along("z", step)
-        pairs = ((st_ref, sts.at[step - 1]), (delta_ref, all_delta_ref.at[z]))
-        for n, (src, dst) in enumerate(pairs):
-            yield pltpu.make_async_remote_copy(
-                src_ref=src,
-                dst_ref=dst,
-                send_sem=st_send.at[step - 1, n],
-                recv_sem=st_recv.at[step - 1, n],
-                device_id=to,
-                device_id_type=MESH,
-            )
-
-    for step in (2, 1, 3):
-        for copy in copies(step):
-            copy.start()
-    all_delta_ref[z] = delta_ref[...]
-    for step in (1, 3, 2):
-        st_copy, delta_copy = copies(step)
-        st_copy.wait()
-        delta_copy.wait_send()
-        ref = all_delta_ref.at[ring_at(z, -step)]
-        pltpu.make_async_remote_copy(
-            src_ref=ref,
-            dst_ref=ref,
-            send_sem=st_send.at[step - 1, 1],
-            recv_sem=st_recv.at[step - 1, 1],
-            device_id=place.along("z", step),
-            device_id_type=MESH,
-        ).wait_recv()
-    top = st_ref[0]
+    )(meta, lists, rows, keys)
+
+
+def merge_statistics(st, sts, total_ref):
+    top = st[0]
     for n in range(3):
         top = jnp.maximum(top, sts[n, 0])
-    total = st_ref[1] * jnp.exp2(st_ref[0] - top)
+    total = st[1] * jnp.exp2(st[0] - top)
     for n in range(3):
         total = total + sts[n, 1] * jnp.exp2(sts[n, 0] - top)
     total_ref[...] = top + jnp.log2(total)
 
 
-def exchange(st, delta):
+def exchange_kernel(st_ref, total_ref, sts, st_send, st_recv):
+    place = Place()
+    greet([place.along("z", step) for step in (1, 2, 3)])
+    copies = [
+        pltpu.make_async_remote_copy(
+            src_ref=st_ref,
+            dst_ref=sts.at[step - 1],
+            send_sem=st_send.at[step - 1],
+            recv_sem=st_recv.at[step - 1],
+            device_id=place.along("z", step),
+            device_id_type=MESH,
+        )
+        for step in (1, 2, 3)
+    ]
+    for copy in copies:
+        copy.start()
+    for copy in copies:
+        copy.wait()
+    merge_statistics(st_ref, sts, total_ref)
+
+
+def exchange(st):
     return pl.pallas_call(
         exchange_kernel,
-        out_shape=(
-            pltpu.VMEM((LOCAL_ROWS, 1, COLS), F32),
-            pltpu.VMEM((RING, QUARTERS, 1, COLS), F32),
-        ),
-        in_specs=[VMEM, VMEM],
-        out_specs=(VMEM, VMEM),
+        out_shape=pltpu.VMEM((LOCAL_ROWS, 1, COLS), F32),
+        in_specs=[VMEM],
+        out_specs=VMEM,
         scratch_shapes=[
             pltpu.VMEM((3, 2, LOCAL_ROWS, 1, COLS), F32),
-            pltpu.SemaphoreType.DMA((3, 2)),
-            pltpu.SemaphoreType.DMA((3, 2)),
+            pltpu.SemaphoreType.DMA((3,)),
+            pltpu.SemaphoreType.DMA((3,)),
         ],
         compiler_params=pltpu.CompilerParams(
             collective_id=1, has_side_effects=True, vmem_limit_bytes=8 * 2**20
         ),
         name="exchange",
-    )(st, delta)
+    )(st)
 
 
 def grads_kernel(
-    task_ref, rows_ref, keys_ref, total_ref, delta_ref, dq_ref, dkv_ref,
-    dq_acc, dk_acc, dv_acc, bias_ref, p_ref, ds_ref,
+    meta_ref, list_ref, rows_ref, keys_ref, total_ref, delta_ref, dq_ref, dkv_ref,
+    task_ref, dq_acc, dk_acc, dv_acc, bias_ref, p_ref, ds_ref,
 ):
+    take_tasks(meta_ref, list_ref, task_ref)
     fill_bias(bias_ref)
     dq_acc[...] = jnp.zeros_like(dq_acc)
     dk_acc[...] = jnp.zeros_like(dk_acc)
@@ -627,16 +706,17 @@
     lax.fori_loop(0, LOCAL_ROWS, write_rows, 0, unroll=8)
 
 
-def grads(tasks, rows, keys, total, delta):
+def grads(meta, lists, rows, keys, total, delta):
     return pl.pallas_call(
         grads_kernel,
         out_shape=(
             pltpu.VMEM((LOCAL_ROWS, PART, D, B), BF),
             pltpu.VMEM((LOCAL_KEYS, 2, B, D), BF),
         ),
-        in_specs=[SMEM] + [VMEM] * 4,
+        in_specs=[SMEM, SMEM] + [VMEM] * 4,
         out_specs=(VMEM, VMEM),
         scratch_shapes=[
+            pltpu.SMEM((TASKS,), jnp.int32),
             pltpu.VMEM((LOCAL_ROWS, D, COLS), F32),
             pltpu.VMEM((LOCAL_KEYS, B, D), F32),
             pltpu.VMEM((LOCAL_KEYS, B, D), F32),
@@ -646,7 +726,7 @@
         ],
         compiler_params=pltpu.CompilerParams(vmem_limit_bytes=32 * 2**20),
         name="grads",
-    )(tasks, rows, keys, total, delta)
+    )(meta, lists, rows, keys, total, delta)
 
 
 class Scatter:
@@ -709,6 +789,16 @@
 
 STEPS = (2, -1, 1, 0)
 MEMBERS = (3, 2, 1, 0)
+ORDER = (
+    "c10P0", "c00F", "c01P1", "c10F", "r0F", "c12F", "r3P1", "r1P0", "c11F",
+    "c01F", "r1P1", "r0P1", "r3F", "c00P0", "c11P0", "c10P1", "c00P1", "c03F",
+    "c12P1", "c02F", "r0P0", "c00W", "c10W", "r3P0", "r2F", "c02P0", "c01P0",
+    "c12P0", "c11P1", "c12W", "c13P1", "c11W", "r0W", "r2P0", "r1F", "r2P1",
+    "c01W", "c10E", "l1F", "c13F", "r2W", "c02W", "c00E", "l0F", "c02P1",
+    "c03W", "r0E", "c03P1", "r3W", "c01E", "l0P1", "c12E", "r1W", "l1P0",
+    "c11E", "l1W", "c13W", "c13P0", "c02E", "l0P0", "c03P0", "l0W", "l1P1",
+    "r1E", "r2E", "c13E", "l1E", "r3E", "c03E", "l0E",
+)
 
 
 def scatter_kernel(
@@ -740,18 +830,6 @@
     rows = [row_ring(k) for k in range(RING)]
     crosses = [[cross(n, k) for k in range(RING)] for n in range(2)]
     lines = [line(n) for n in range(2)]
-    waves = [(crosses[0][k], crosses[1][k], rows[k]) for k in range(RING)]
-    for wave in waves:
-        for ring in wave:
-            ring.start_far()
-    for wave in waves:
-        for ring in wave:
-            for way in range(2):
-                ring.start_plain(way)
-    for wave in waves:
-        for ring in wave:
-            ring.forward()
-
     part_cols = pl.ds(pl.multiple_of(place.quarter(0) * COLS, COLS), COLS)
 
     def q_copy(k):
@@ -766,31 +844,6 @@
         )
 
     q_own = pltpu.make_async_copy(qout.at[RING - 1], qg_ref.at[:, part_cols], local.at[0])
-    for k in range(RING):
-        for n in range(2):
-            ring = crosses[n][k]
-            ring.finish()
-            for half in range(2):
-                total = ring.total(half)
-                if STEPS[k] == 0:
-                    own_sum[n, half] = total
-                else:
-                    sums[n, ring_at((x, y)[n], STEPS[k]), half] = total.astype(BF)
-            if STEPS[k] == 2:
-                lines[n].start_far()
-            elif STEPS[k] != 0:
-                lines[n].start_plain(0 if STEPS[k] == 1 else 1)
-        if k == 2:
-            for n in range(2):
-                lines[n].forward()
-        rows[k].finish()
-        for half in range(PART):
-            qout[k, :, half * D : (half + 1) * D] = jnp.transpose(rows[k].total(half)).astype(BF)
-        if MEMBERS[k]:
-            q_copy(k).start()
-        else:
-            q_own.start()
-
     ours = pl.ds(pl.multiple_of(h * D, D), D)
     theirs = pl.ds(pl.multiple_of((1 - h) * D, D), D)
     swaps = [
@@ -808,12 +861,44 @@
         pltpu.make_async_copy(fin.at[0, n], target.at[:, ours], local.at[1 + n])
         for n, target in enumerate((kg_ref, vg_ref))
     ]
-    for n, copies in ((1, swaps), (0, outs)):
+    def end_rows(k):
+        rows[k].finish()
+        for half in range(PART):
+            qout[k, :, half * D : (half + 1) * D] = jnp.transpose(rows[k].total(half)).astype(BF)
+        if MEMBERS[k]:
+            q_copy(k).start()
+        else:
+            q_own.start()
+
+    def end_cross(n, k):
+        ring = crosses[n][k]
+        ring.finish()
+        for half in range(2):
+            total = ring.total(half)
+            if STEPS[k] == 0:
+                own_sum[n, half] = total
+            else:
+                sums[n, ring_at((x, y)[n], STEPS[k]), half] = total.astype(BF)
+
+    def end_line(n):
         lines[n].finish()
         for half in range(2):
             fin[n, half] = lines[n].total(half, own_sum[n, half]).astype(BF)
-        for copy in copies:
+        for copy in (outs, swaps)[n]:
             copy.start()
+
+    for step in ORDER:
+        at = [int(c) for c in step if c.isdigit()]
+        kind, action = step[0], next(c for c in step if c in "FPWE")
+        ring = {"r": lambda: rows[at[0]], "c": lambda: crosses[at[0]][at[1]], "l": lambda: lines[at[0]]}[kind]()
+        if action == "F":
+            ring.start_far()
+        elif action == "P":
+            ring.start_plain(at[-1])
+        elif action == "W":
+            ring.forward()
+        else:
+            {"r": end_rows, "c": end_cross, "l": end_line}[kind](*at)
     for copy in outs:
         copy.wait()
     q_own.wait()
@@ -914,12 +999,11 @@
 
 
 def body(q, k, v, o, g, query_blocks, key_blocks, kept_blocks):
-    rows, keys, delta, meta = gather(query_blocks, key_blocks, kept_blocks, q, k, v, o, g)
+    rows, keys, delta, meta, lists = gather(query_blocks, key_blocks, kept_blocks, q, k, v, o, g)
     rows = rows.reshape(LOCAL_ROWS, 2, PART, B, D)
     keys = keys.reshape(LOCAL_KEYS, 2, B, D)
-    st, tasks = statistics(meta, rows, keys)
-    total, all_delta = exchange(st, delta)
-    dq, dkv = grads(tasks, rows, keys, total, all_delta.reshape(LOCAL_ROWS, 1, COLS))
+    total = exchange(statistics(meta, lists, rows, keys))
+    dq, dkv = grads(meta, lists, rows, keys, total, delta.reshape(LOCAL_ROWS, 1, COLS))
     return store(*scatter(dq, dkv))
 
 

time: 69.6 us -> 71.3 us (1.024)
  Pallas kernels: 68.8 us -> 70.4 us
    pallas_call x1, Pallas kernels: 30 us -> 24.5 us  [scatter(): pl.pallas_call(scatter_kernel, out_shape=(pltpu.VMEM((B, HEADS * D), BF),...]
    pallas_call x1, Pallas kernels: 4.3 us -> 8.83 us  [grads(): pl.pallas_call(grads_kernel, out_shape=(pltpu.VMEM((LOCAL_ROWS, PART, D,...]
    pallas_call x2, Pallas kernels: 7.8 us -> 9.49 us  [the longest x1 4.99 us: exchange(): pl.pallas_call(exchange_kernel, out_shape=pltpu.VMEM((LOCAL_ROWS, 1, COLS...]
    pallas_call x1, Pallas kernels: 26 us -> 26.9 us  [gather(): pl.pallas_call(gather_kernel, out_shape=(pltpu.VMEM((RING, QUARTERS, 2, P...]
where the time goes in v3:
time: 71.3 us; the launch traced here: 71.1 us
  Pallas kernels  70.4 us (99%)
    pallas_call x1, Pallas kernels, gather(): pl.pallas_call(gather_kernel, out_shape=(pltpu.VMEM((RING, QUARTERS, 2, P...  26.9 us
    pallas_call x1, Pallas kernels, scatter(): pl.pallas_call(scatter_kernel, out_shape=(pltpu.VMEM((B, HEADS * D), BF),...  24.5 us
    pallas_call x1, Pallas kernels, grads(): pl.pallas_call(grads_kernel, out_shape=(pltpu.VMEM((LOCAL_ROWS, PART, D,...  8.83 us
    pallas_call x1, Pallas kernels, exchange(): pl.pallas_call(exchange_kernel, out_shape=pltpu.VMEM((LOCAL_ROWS, 1, COLS...  4.99 us
    pallas_call x1, Pallas kernels, statistics(): pl.pallas_call(stats_kernel, out_shape=pltpu.VMEM((2, LOCAL_ROWS, 1, COLS...  4.5 us

profile of v3, /device:TPU:1, one launch (start us, length us, event | category | flops | bytes accessed | tf_op | source)
XLA Modules:
  0.0 71.1 jit_solution(1695013470689479541)
XLA Ops:
  0.6 26.9 %gather.1 = (bf16[4,4,2,2,128,128]{5,4,3,2,1,0:T(8,128)(2,1)S(1)}, bf16[2,4,4,2,128,128]{5,4,3,2,1,0:T(8,128)(2,1)S(1)}, f32[4,4,1,256]{3,2,1,0:T(1,128)S(1)}, s32[16,128]{1,0:T(8,128)S(1)}, s32[8,128]{1,0:T(8,128)S(1)}) custom-call(s32[64]{0:T(128)} %qb_hbm.1, s32[128]{0:T(128)} %kb_hbm.1, s32[64,64]{1,0:T(8,128)} %kept_hbm.1, bf16[128,1024]{1,0:T(8,128)(2,1)} %q_ref.1, ...), custom_call_target="tpu_custom_call" | custom-call | tf_op jit(solution)/shard_map/gather/pallas_call | solution.py:457
  27.5 4.5 %statistics.1.st_ref = f32[2,16,1,256]{3,2,1,0:T(1,128)S(1)} custom-call(s32[16,128]{1,0:T(8,128)S(1)} %get-tuple-element.13.meta_ref, s32[8,128]{1,0:T(8,128)S(1)} %get-tuple-element.14.list_ref, bf16[16,2,2,128,128]{4,3,2,1,0:T(8,128)(2,1)S(1)} %bitcast.5, bf16[32,2,128,128]{3,2,1,0:T(8,128)(2,1)S(1)} %bitcast.7), custom_call_target="tpu_custom_call" | custom-call | tf_op jit(solution)/shard_map/statistics/pallas_call | solution.py:594
  32.0 5.0 %exchange.1.total_ref = f32[16,1,256]{2,1,0:T(1,128)S(1)} custom-call(f32[2,16,1,256]{3,2,1,0:T(1,128)S(1)} %statistics.1.st_ref), custom_call_target="tpu_custom_call" | custom-call | tf_op jit(solution)/shard_map/exchange/pallas_call | solution.py:642
  37.0 8.8 %grads.1 = (bf16[16,2,128,128]{3,2,1,0:T(8,128)(2,1)S(1)}, bf16[32,2,128,128]{3,2,1,0:T(8,128)(2,1)S(1)}) custom-call(s32[16,128]{1,0:T(8,128)S(1)} %get-tuple-element.13.meta_ref, s32[8,128]{1,0:T(8,128)S(1)} %get-tuple-element.14.list_ref, bf16[16,2,2,128,128]{4,3,2,1,0:T(8,128)(2,1)S(1)} %bitcast.6, bf16[32,2,128,128]{3,2,1,0:T(8,128)(2,1)S(1)} %bitcast.8, ...), custom_call_target="tpu_custom_call" | custom-call | tf_op jit(solution)/shard_map/grads/pallas_call | solution.py:710
  45.9 24.5 %scatter.1 = (bf16[128,1024]{1,0:T(8,128)(2,1)S(1)}, bf16[128,256]{1,0:T(8,128)(2,1)S(1)}, bf16[128,256]{1,0:T(8,128)(2,1)S(1)}) custom-call(bf16[4,4,2,128,128]{4,3,2,1,0:T(8,128)(2,1)S(1)} %bitcast.10, bf16[2,4,4,2,128,128]{5,4,3,2,1,0:T(8,128)(2,1)S(1)} %bitcast.9), custom_call_target="tpu_custom_call" | custom-call | tf_op jit(solution)/shard_map/scatter/pallas_call | solution.py:943
  70.4 0.8 %store.1 = (bf16[128,1024]{1,0:T(8,128)(2,1)}, bf16[128,256]{1,0:T(8,128)(2,1)}, bf16[128,256]{1,0:T(8,128)(2,1)}) custom-call(bf16[128,1024]{1,0:T(8,128)(2,1)S(1)} %get-tuple-element.20.q_ref, bf16[128,256]{1,0:T(8,128)(2,1)S(1)} %get-tuple-element.21.k_ref, bf16[128,256]{1,0:T(8,128)(2,1)S(1)} %get-tuple-element.22.v_ref), custom_call_target="tpu_custom_call" | custom-call | tf_op jit(solution)/shard_map/store/pallas_call | solution.py:990

commit v4 on v3

--- a/solution.py
+++ b/solution.py
@@ -19,7 +19,7 @@
 ENTRIES = 64
 GROUP = 8
 TASKS = 272
-EARLY = 120
+EARLY = 64
 FIRST_KEY = 64
 SCALE = 1.0 / math.sqrt(D)
 LOG2E = math.log2(math.e)
@@ -545,7 +545,7 @@
     )
 
 
-def take_tasks(meta_ref, list_ref, task_ref):
+def take_tasks(meta_hbm, list_ref, task_ref, meta_ref, meta_sem):
     count = list_ref[1, 0]
 
     @pl.when(count <= EARLY)
@@ -556,11 +556,16 @@
 
     @pl.when(count > EARLY)
     def _():
+        copy = pltpu.make_async_copy(meta_hbm, meta_ref, meta_sem)
+        copy.start()
+        copy.wait()
         list_tasks(meta_ref, task_ref)
 
 
-def stats_kernel(meta_ref, list_ref, rows_ref, keys_ref, st_ref, task_ref, m_ref, l_ref, bias_ref):
-    take_tasks(meta_ref, list_ref, task_ref)
+def stats_kernel(
+    meta_hbm, list_ref, rows_ref, keys_ref, st_ref, task_ref, meta_ref, meta_sem, m_ref, l_ref, bias_ref
+):
+    take_tasks(meta_hbm, list_ref, task_ref, meta_ref, meta_sem)
     fill_bias(bias_ref)
     m_ref[...] = jnp.full_like(m_ref, NEG)
     l_ref[...] = jnp.zeros_like(l_ref)
@@ -586,18 +591,20 @@
     lax.fori_loop(0, task_ref[TASKS - 1], group, 0)
     m8 = m_ref[...]
     m = jnp.max(m8, axis=1, keepdims=True)
-    st_ref[0] = m
-    st_ref[1] = jnp.sum(l_ref[...] * jnp.exp2(m8 - m), axis=1, keepdims=True)
+    l = jnp.sum(l_ref[...] * jnp.exp2(m8 - m), axis=1, keepdims=True)
+    st_ref[...] = jnp.where(l > 0.0, m + jnp.log2(l), NEG)
 
 
 def statistics(meta, lists, rows, keys):
     return pl.pallas_call(
         stats_kernel,
-        out_shape=pltpu.VMEM((2, LOCAL_ROWS, 1, COLS), F32),
-        in_specs=[SMEM, SMEM, VMEM, VMEM],
+        out_shape=pltpu.VMEM((LOCAL_ROWS, 1, COLS), F32),
+        in_specs=[ANY, SMEM, VMEM, VMEM],
         out_specs=VMEM,
         scratch_shapes=[
             pltpu.SMEM((TASKS,), jnp.int32),
+            pltpu.SMEM((LOCAL_ROWS, 128), jnp.int32),
+            pltpu.SemaphoreType.DMA,
             pltpu.VMEM((LOCAL_ROWS, 8, COLS), F32),
             pltpu.VMEM((LOCAL_ROWS, 8, COLS), F32),
             pltpu.VMEM((3, B, COLS), F32),
@@ -605,16 +612,6 @@
         compiler_params=pltpu.CompilerParams(vmem_limit_bytes=24 * 2**20),
         name="statistics",
     )(meta, lists, rows, keys)
-
-
-def merge_statistics(st, sts, total_ref):
-    top = st[0]
-    for n in range(3):
-        top = jnp.maximum(top, sts[n, 0])
-    total = st[1] * jnp.exp2(st[0] - top)
-    for n in range(3):
-        total = total + sts[n, 1] * jnp.exp2(sts[n, 0] - top)
-    total_ref[...] = top + jnp.log2(total)
 
 
 def exchange_kernel(st_ref, total_ref, sts, st_send, st_recv):
@@ -635,7 +632,9 @@
         copy.start()
     for copy in copies:
         copy.wait()
-    merge_statistics(st_ref, sts, total_ref)
+    logs = [st_ref[...]] + [sts[n] for n in range(3)]
+    top = jnp.maximum(jnp.maximum(logs[0], logs[1]), jnp.maximum(logs[2], logs[3]))
+    total_ref[...] = top + jnp.log2(sum(jnp.exp2(log - top) for log in logs))
 
 
 def exchange(st):
@@ -645,7 +644,7 @@
         in_specs=[VMEM],
         out_specs=VMEM,
         scratch_shapes=[
-            pltpu.VMEM((3, 2, LOCAL_ROWS, 1, COLS), F32),
+            pltpu.VMEM((3, LOCAL_ROWS, 1, COLS), F32),
             pltpu.SemaphoreType.DMA((3,)),
             pltpu.SemaphoreType.DMA((3,)),
         ],
@@ -657,10 +656,10 @@
 
 
 def grads_kernel(
-    meta_ref, list_ref, rows_ref, keys_ref, total_ref, delta_ref, dq_ref, dkv_ref,
-    task_ref, dq_acc, dk_acc, dv_acc, bias_ref, p_ref, ds_ref,
+    meta_hbm, list_ref, rows_ref, keys_ref, total_ref, delta_ref, dq_ref, dkv_ref,
+    task_ref, meta_ref, meta_sem, dq_acc, dk_acc, dv_acc, bias_ref, p_ref, ds_ref,
 ):
-    take_tasks(meta_ref, list_ref, task_ref)
+    take_tasks(meta_hbm, list_ref, task_ref, meta_ref, meta_sem)
     fill_bias(bias_ref)
     dq_acc[...] = jnp.zeros_like(dq_acc)
     dk_acc[...] = jnp.zeros_like(dk_acc)
@@ -713,10 +712,12 @@
             pltpu.VMEM((LOCAL_ROWS, PART, D, B), BF),
             pltpu.VMEM((LOCAL_KEYS, 2, B, D), BF),
         ),
-        in_specs=[SMEM, SMEM] + [VMEM] * 4,
+        in_specs=[ANY, SMEM] + [VMEM] * 4,
         out_specs=(VMEM, VMEM),
         scratch_shapes=[
             pltpu.SMEM((TASKS,), jnp.int32),
+            pltpu.SMEM((LOCAL_ROWS, 128), jnp.int32),
+            pltpu.SemaphoreType.DMA,
             pltpu.VMEM((LOCAL_ROWS, D, COLS), F32),
             pltpu.VMEM((LOCAL_KEYS, B, D), F32),
             pltpu.VMEM((LOCAL_KEYS, B, D), F32),

time: 71.3 us -> 68 us (0.954)
  Pallas kernels: 70.4 us -> 67.2 us
    pallas_call x1, Pallas kernels: 8.83 us -> 4.38 us  [grads(): pl.pallas_call(grads_kernel, out_shape=(pltpu.VMEM((LOCAL_ROWS, PART, D,...]
    pallas_call x1, Pallas kernels: 24.5 us -> 28.3 us  [scatter(): pl.pallas_call(scatter_kernel, out_shape=(pltpu.VMEM((B, HEADS * D), BF),...]
    pallas_call x1, Pallas kernels: 4.5 us -> 2.24 us  [statistics(): pl.pallas_call(stats_kernel, out_shape=pltpu.VMEM((LOCAL_ROWS, 1, COLS),...]
where the time goes in v4:
time: 68 us; the launch traced here: 67.9 us
  Pallas kernels  67.2 us (99%)
    pallas_call x1, Pallas kernels, scatter(): pl.pallas_call(scatter_kernel, out_shape=(pltpu.VMEM((B, HEADS * D), BF),...  28.3 us
    pallas_call x1, Pallas kernels, gather(): pl.pallas_call(gather_kernel, out_shape=(pltpu.VMEM((RING, QUARTERS, 2, P...  26.9 us
    pallas_call x1, Pallas kernels, exchange(): pl.pallas_call(exchange_kernel, out_shape=pltpu.VMEM((LOCAL_ROWS, 1, COLS...  4.64 us
    pallas_call x1, Pallas kernels, grads(): pl.pallas_call(grads_kernel, out_shape=(pltpu.VMEM((LOCAL_ROWS, PART, D,...  4.38 us
    pallas_call x1, Pallas kernels, statistics(): pl.pallas_call(stats_kernel, out_shape=pltpu.VMEM((LOCAL_ROWS, 1, COLS),...  2.24 us

profile of v4, /device:TPU:1, one launch (start us, length us, event | category | flops | bytes accessed | tf_op | source)
XLA Modules:
  0.0 67.9 jit_solution(9529673393564012284)
XLA Ops:
  0.6 26.9 %gather.1 = (bf16[4,4,2,2,128,128]{5,4,3,2,1,0:T(8,128)(2,1)S(1)}, bf16[2,4,4,2,128,128]{5,4,3,2,1,0:T(8,128)(2,1)S(1)}, f32[4,4,1,256]{3,2,1,0:T(1,128)S(1)}, s32[16,128]{1,0:T(8,128)S(1)}, s32[8,128]{1,0:T(8,128)S(1)}) custom-call(s32[64]{0:T(128)} %qb_hbm.1, s32[128]{0:T(128)} %kb_hbm.1, s32[64,64]{1,0:T(8,128)} %kept_hbm.1, bf16[128,1024]{1,0:T(8,128)(2,1)} %q_ref.1, ...), custom_call_target="tpu_custom_call" | custom-call | tf_op jit(solution)/shard_map/gather/pallas_call | solution.py:457
  27.5 2.2 %statistics.1.st_ref = f32[16,1,256]{2,1,0:T(1,128)S(1)} custom-call(s32[16,128]{1,0:T(8,128)S(1)} %get-tuple-element.13.meta_hbm, s32[8,128]{1,0:T(8,128)S(1)} %get-tuple-element.14.list_ref, bf16[16,2,2,128,128]{4,3,2,1,0:T(8,128)(2,1)S(1)} %bitcast.5, bf16[32,2,128,128]{3,2,1,0:T(8,128)(2,1)S(1)} %bitcast.7), custom_call_target="tpu_custom_call" | custom-call | tf_op jit(solution)/shard_map/statistics/pallas_call | solution.py:599
  29.8 4.6 %exchange.1.total_ref = f32[16,1,256]{2,1,0:T(1,128)S(1)} custom-call(f32[16,1,256]{2,1,0:T(1,128)S(1)} %statistics.1.st_ref), custom_call_target="tpu_custom_call" | custom-call | tf_op jit(solution)/shard_map/exchange/pallas_call | solution.py:641
  34.4 4.4 %grads.1 = (bf16[16,2,128,128]{3,2,1,0:T(8,128)(2,1)S(1)}, bf16[32,2,128,128]{3,2,1,0:T(8,128)(2,1)S(1)}) custom-call(s32[16,128]{1,0:T(8,128)S(1)} %get-tuple-element.13.meta_hbm, s32[8,128]{1,0:T(8,128)S(1)} %get-tuple-element.14.list_ref, bf16[16,2,2,128,128]{4,3,2,1,0:T(8,128)(2,1)S(1)} %bitcast.6, bf16[32,2,128,128]{3,2,1,0:T(8,128)(2,1)S(1)} %bitcast.8, ...), custom_call_target="tpu_custom_call" | custom-call | tf_op jit(solution)/shard_map/grads/pallas_call | solution.py:709
  38.8 28.3 %scatter.1 = (bf16[128,1024]{1,0:T(8,128)(2,1)S(1)}, bf16[128,256]{1,0:T(8,128)(2,1)S(1)}, bf16[128,256]{1,0:T(8,128)(2,1)S(1)}) custom-call(bf16[4,4,2,128,128]{4,3,2,1,0:T(8,128)(2,1)S(1)} %bitcast.10, bf16[2,4,4,2,128,128]{5,4,3,2,1,0:T(8,128)(2,1)S(1)} %bitcast.9), custom_call_target="tpu_custom_call" | custom-call | tf_op jit(solution)/shard_map/scatter/pallas_call | solution.py:944
  67.1 0.8 %store.1 = (bf16[128,1024]{1,0:T(8,128)(2,1)}, bf16[128,256]{1,0:T(8,128)(2,1)}, bf16[128,256]{1,0:T(8,128)(2,1)}) custom-call(bf16[128,1024]{1,0:T(8,128)(2,1)S(1)} %get-tuple-element.20.q_ref, bf16[128,256]{1,0:T(8,128)(2,1)S(1)} %get-tuple-element.21.k_ref, bf16[128,256]{1,0:T(8,128)(2,1)S(1)} %get-tuple-element.22.v_ref), custom_call_target="tpu_custom_call" | custom-call | tf_op jit(solution)/shard_map/store/pallas_call | solution.py:991

commit v5 on v4

--- a/solution.py
+++ b/solution.py
@@ -531,7 +531,7 @@
     count = lax.fori_loop(0, LOCAL_ROWS, row, jnp.int32(0))
     for n in range(GROUP - 1):
         task_ref[count + n] = 0
-    task_ref[TASKS - 1] = (count + GROUP - 1) // GROUP
+    task_ref[TASKS - 1] = count
 
 
 def read_task(task_ref, n):
@@ -552,7 +552,7 @@
     def _():
         for n in range(EARLY):
             task_ref[n] = list_ref[0, n]
-        task_ref[TASKS - 1] = (count + GROUP - 1) // GROUP
+        task_ref[TASKS - 1] = count
 
     @pl.when(count > EARLY)
     def _():
@@ -560,6 +560,22 @@
         copy.start()
         copy.wait()
         list_tasks(meta_ref, task_ref)
+
+
+def in_groups(task_ref, work):
+    count = task_ref[TASKS - 1]
+    rest = lax.rem(count, GROUP)
+    whole = count // GROUP + (rest > GROUP // 2).astype(jnp.int32)
+
+    def group(n, _):
+        work(GROUP * n, GROUP)
+        return 0
+
+    lax.fori_loop(0, whole, group, 0)
+
+    @pl.when((rest > 0) & (rest <= GROUP // 2))
+    def _():
+        work(GROUP * whole, GROUP // 2)
 
 
 def stats_kernel(
@@ -570,10 +586,10 @@
     m_ref[...] = jnp.full_like(m_ref, NEG)
     l_ref[...] = jnp.zeros_like(l_ref)
 
-    def group(n, _):
+    def work(first, size):
         results = []
-        for t in range(GROUP):
-            i, j0, j1, kind0, kind1 = read_task(task_ref, GROUP * n + t)
+        for t in range(size):
+            i, j0, j1, kind0, kind1 = read_task(task_ref, first + t)
             queries = rows_ref[i, 0].reshape(COLS, D)
             keys = jnp.concatenate([keys_ref[j0, 0], keys_ref[j1, 0]], axis=0)
             s = across(keys, queries) * C2
@@ -586,9 +602,8 @@
             new = jnp.maximum(old, m)
             m_ref[i] = new
             l_ref[i] = l_ref[i] * jnp.exp2(old - new) + l * jnp.exp2(m - new)
-        return 0
-
-    lax.fori_loop(0, task_ref[TASKS - 1], group, 0)
+
+    in_groups(task_ref, work)
     m8 = m_ref[...]
     m = jnp.max(m8, axis=1, keepdims=True)
     l = jnp.sum(l_ref[...] * jnp.exp2(m8 - m), axis=1, keepdims=True)
@@ -665,8 +680,8 @@
     dk_acc[...] = jnp.zeros_like(dk_acc)
     dv_acc[...] = jnp.zeros_like(dv_acc)
 
-    def group(n, _):
-        tasks = [read_task(task_ref, GROUP * n + t) for t in range(GROUP)]
+    def work(first, size):
+        tasks = [read_task(task_ref, first + t) for t in range(size)]
         for t, (i, j0, j1, kind0, kind1) in enumerate(tasks):
             keys = jnp.concatenate([keys_ref[j0, 0], keys_ref[j1, 0]], axis=0)
             values = jnp.concatenate([keys_ref[j0, 1], keys_ref[j1, 1]], axis=0)
@@ -686,9 +701,8 @@
             dk_acc[j1] += dk[B:]
             dv_acc[j0] += dv[:B]
             dv_acc[j1] += dv[B:]
-        return 0
-
-    lax.fori_loop(0, task_ref[TASKS - 1], group, 0)
+
+    in_groups(task_ref, work)
 
     def write(j, _):
         dkv_ref[j, 0] = (dk_acc[j] * SCALE).astype(BF)

time: 68 us -> 70.4 us (1.035)
  Pallas kernels: 67.2 us -> 69.6 us
    pallas_call x1, Pallas kernels: 28.3 us -> 30.8 us  [scatter(): pl.pallas_call(scatter_kernel, out_shape=(pltpu.VMEM((B, HEADS * D), BF),...]
where the time goes in v5:
time: 70.4 us; the launch traced here: 70.3 us
  Pallas kernels  69.6 us (99%)
    pallas_call x1, Pallas kernels, scatter(): pl.pallas_call(scatter_kernel, out_shape=(pltpu.VMEM((B, HEADS * D), BF),...  30.8 us
    pallas_call x1, Pallas kernels, gather(): pl.pallas_call(gather_kernel, out_shape=(pltpu.VMEM((RING, QUARTERS, 2, P...  26.9 us
    pallas_call x1, Pallas kernels, exchange(): pl.pallas_call(exchange_kernel, out_shape=pltpu.VMEM((LOCAL_ROWS, 1, COLS...  4.5 us
    pallas_call x1, Pallas kernels, grads(): pl.pallas_call(grads_kernel, out_shape=(pltpu.VMEM((LOCAL_ROWS, PART, D,...  4.4 us
    pallas_call x1, Pallas kernels, statistics(): pl.pallas_call(stats_kernel, out_shape=pltpu.VMEM((LOCAL_ROWS, 1, COLS),...  2.23 us

profile of v5, /device:TPU:1, one launch (start us, length us, event | category | flops | bytes accessed | tf_op | source)
XLA Modules:
  0.0 70.3 jit_solution(6166518484499608613)
XLA Ops:
  0.6 26.9 %gather.1 = (bf16[4,4,2,2,128,128]{5,4,3,2,1,0:T(8,128)(2,1)S(1)}, bf16[2,4,4,2,128,128]{5,4,3,2,1,0:T(8,128)(2,1)S(1)}, f32[4,4,1,256]{3,2,1,0:T(1,128)S(1)}, s32[16,128]{1,0:T(8,128)S(1)}, s32[8,128]{1,0:T(8,128)S(1)}) custom-call(s32[64]{0:T(128)} %qb_hbm.1, s32[128]{0:T(128)} %kb_hbm.1, s32[64,64]{1,0:T(8,128)} %kept_hbm.1, bf16[128,1024]{1,0:T(8,128)(2,1)} %q_ref.1, ...), custom_call_target="tpu_custom_call" | custom-call | tf_op jit(solution)/shard_map/gather/pallas_call | solution.py:457
  27.5 2.2 %statistics.1.st_ref = f32[16,1,256]{2,1,0:T(1,128)S(1)} custom-call(s32[16,128]{1,0:T(8,128)S(1)} %get-tuple-element.13.meta_hbm, s32[8,128]{1,0:T(8,128)S(1)} %get-tuple-element.14.list_ref, bf16[16,2,2,128,128]{4,3,2,1,0:T(8,128)(2,1)S(1)} %bitcast.5, bf16[32,2,128,128]{3,2,1,0:T(8,128)(2,1)S(1)} %bitcast.7), custom_call_target="tpu_custom_call" | custom-call | tf_op jit(solution)/shard_map/statistics/pallas_call | solution.py:614
  29.8 4.5 %exchange.1.total_ref = f32[16,1,256]{2,1,0:T(1,128)S(1)} custom-call(f32[16,1,256]{2,1,0:T(1,128)S(1)} %statistics.1.st_ref), custom_call_target="tpu_custom_call" | custom-call | tf_op jit(solution)/shard_map/exchange/pallas_call | solution.py:656
  34.3 4.4 %grads.1 = (bf16[16,2,128,128]{3,2,1,0:T(8,128)(2,1)S(1)}, bf16[32,2,128,128]{3,2,1,0:T(8,128)(2,1)S(1)}) custom-call(s32[16,128]{1,0:T(8,128)S(1)} %get-tuple-element.13.meta_hbm, s32[8,128]{1,0:T(8,128)S(1)} %get-tuple-element.14.list_ref, bf16[16,2,2,128,128]{4,3,2,1,0:T(8,128)(2,1)S(1)} %bitcast.6, bf16[32,2,128,128]{3,2,1,0:T(8,128)(2,1)S(1)} %bitcast.8, ...), custom_call_target="tpu_custom_call" | custom-call | tf_op jit(solution)/shard_map/grads/pallas_call | solution.py:723
  38.7 30.8 %scatter.1 = (bf16[128,1024]{1,0:T(8,128)(2,1)S(1)}, bf16[128,256]{1,0:T(8,128)(2,1)S(1)}, bf16[128,256]{1,0:T(8,128)(2,1)S(1)}) custom-call(bf16[4,4,2,128,128]{4,3,2,1,0:T(8,128)(2,1)S(1)} %bitcast.10, bf16[2,4,4,2,128,128]{5,4,3,2,1,0:T(8,128)(2,1)S(1)} %bitcast.9), custom_call_target="tpu_custom_call" | custom-call | tf_op jit(solution)/shard_map/scatter/pallas_call | solution.py:958
  69.5 0.8 %store.1 = (bf16[128,1024]{1,0:T(8,128)(2,1)}, bf16[128,256]{1,0:T(8,128)(2,1)}, bf16[128,256]{1,0:T(8,128)(2,1)}) custom-call(bf16[128,1024]{1,0:T(8,128)(2,1)S(1)} %get-tuple-element.20.q_ref, bf16[128,256]{1,0:T(8,128)(2,1)S(1)} %get-tuple-element.21.k_ref, bf16[128,256]{1,0:T(8,128)(2,1)S(1)} %get-tuple-element.22.v_ref), custom_call_target="tpu_custom_call" | custom-call | tf_op jit(solution)/shard_map/store/pallas_call | solution.py:1005
